TPU v7x, 32 devices: a whole 2x2x4 slice. The times are simulated.
32 devices in a mesh: win: 8 (over z, x), grp: 4 (over y, core).
Axes of the slice: x: 2, y: 2, z: 4, core: 2. Of those that a mesh axis runs over, the one named last changes fastest.
Arguments:
- x_slots: bfloat16 [160, 196, 768], P(('win', 'grp')), may hold values from -6 to 6
- counts: int32 [32], P(('win', 'grp')), may hold values from 1 to 5, as said below
- cotangent: bfloat16 [96, 196, 768], P(('win', 'grp')), may hold values from -6 to 6
- w_qkv: bfloat16 [768, 2304], replicated, may hold values from -0.21875 to 0.21875
- w_proj: bfloat16 [768, 768], replicated, may hold values from -0.875 to 0.875
- w_fc1: bfloat16 [768, 3072], replicated, may hold values from -0.21875 to 0.21875
- w_fc2: bfloat16 [3072, 768], replicated, may hold values from -0.109375 to 0.109375
- small_params: bfloat16 [12672], replicated, may hold values from -1.5 to 1.5
- moment_qkv: float32 [768, 2304], P('win', 'grp'), may hold values from -64 to 64
- moment_proj: float32 [768, 768], P('win', 'grp'), may hold values from -64 to 64
- moment_fc1: float32 [768, 3072], P('win', 'grp'), may hold values from -64 to 64
- moment_fc2: float32 [3072, 768], P('win', 'grp'), may hold values from -64 to 64
- moment_small: float32 [12672], replicated, may hold values from -64 to 64
- square_qkv: float32 [768, 2304], P('win', 'grp'), may hold values from 1 to 96
- square_proj: float32 [768, 768], P('win', 'grp'), may hold values from 1 to 96
- square_fc1: float32 [768, 3072], P('win', 'grp'), may hold values from 1 to 96
- square_fc2: float32 [3072, 768], P('win', 'grp'), may hold values from 1 to 96
- square_small: float32 [12672], replicated, may hold values from 1 to 96
Outputs:
- block_out: bfloat16 [96, 196, 768], P(('win', 'grp'))
- input_grad: bfloat16 [160, 196, 768], P(('win', 'grp'))
- grad_qkv: float32 [768, 2304], P('win', 'grp')
- grad_proj: float32 [768, 768], P('win', 'grp')
- grad_fc1: float32 [768, 3072], P('win', 'grp')
- grad_fc2: float32 [3072, 768], P('win', 'grp')
- grad_small: float32 [12672], replicated
- next_moment_qkv: float32 [768, 2304], P('win', 'grp')
- next_moment_proj: float32 [768, 768], P('win', 'grp')
- next_moment_fc1: float32 [768, 3072], P('win', 'grp')
- next_moment_fc2: float32 [3072, 768], P('win', 'grp')
- next_moment_small: float32 [12672], replicated
- next_square_qkv: float32 [768, 2304], P('win', 'grp')
- next_square_proj: float32 [768, 768], P('win', 'grp')
- next_square_fc1: float32 [768, 3072], P('win', 'grp')
- next_square_fc2: float32 [3072, 768], P('win', 'grp')
- next_square_small: float32 [12672], replicated
- new_qkv: bfloat16 [768, 2304], P(None, 'grp')
- new_proj: bfloat16 [768, 768], P(None, 'grp')
- new_fc1: bfloat16 [768, 3072], P(None, 'grp')
- new_fc2: bfloat16 [3072, 768], P(None, 'grp')
- new_small: bfloat16 [12672], replicated
Inputs may be any that keep to these rules, and one draw needn't show every extreme that they name: Device d holds the windows offset_d to offset_d + counts_d - 1, offset_d being the sum of the counts before it; offset_d differs from 3 * d by exactly one for 0 < d < 32, and the counts add up to 96.
All inputs are finite; a program needn't handle non-finite values.
Results may differ from a plain program's by a relative error of at most 0.017.
Values may be sent and summed in bfloat16 or wider, within the bound.
No kernel may reach another device: no remote copies, remote signals or barrier semaphores. Data moves between devices by JAX's collectives and lax.ppermute only.
A program may use at most 448 MiB of HBM per device.

v0:
```python
import jax
import jax.numpy as jnp
from jax import lax
from jax.sharding import PartitionSpec as P

D = 768
HEADS = 12
HD = 64
FF = 3072
WS = 14
SIDE = 64
STEP = 4
TOKW = 196
GRID = 5
RELN = 27


precise = lax.Precision.HIGHEST
root_half = 0.7071067811865476
inv_root_two_pi = 0.3989422804014327
learn_rate = 0.06


def entering(part, axis, combine, identity):
    place = lax.axis_index(axis)
    gathered = lax.all_gather(part, axis)
    state = jnp.zeros_like(part) + jnp.asarray(identity, part.dtype)

    def one(step, state):
        return combine(state, lax.dynamic_index_in_dim(gathered, step, 0, False))

    return lax.fori_loop(0, place, one, state)


def padded(array, sides, width):
    for axis, dim in sides:
        peers, length = (lax.axis_size(axis), array.shape[dim])
        up = [(i, (i + 1) % peers) for i in range(peers - 1)]
        down = [(j, i) for i, j in up]
        last = lax.slice_in_dim(array, length - width, length, axis=dim)
        first = lax.slice_in_dim(array, 0, width, axis=dim)
        before = lax.ppermute(last, axis, up)
        after = lax.ppermute(first, axis, down)
        array = jnp.concatenate([before, array, after], axis=dim)
    return array


def unpack(small):
    gain_one = small[0:D]
    gain_two = small[D : 2 * D]
    shift_one = small[2 * D : 3 * D]
    shift_two = small[3 * D : 4 * D]
    query_bias = small[4 * D : 5 * D]
    value_bias = small[5 * D : 6 * D]
    proj_bias = small[6 * D : 7 * D]
    second_bias = small[7 * D : 8 * D]
    first_bias = small[8 * D : 8 * D + FF]
    tables = small[8 * D + FF :].reshape(2, RELN, HD)
    return (
        gain_one,
        gain_two,
        shift_one,
        shift_two,
        query_bias,
        value_bias,
        proj_bias,
        second_bias,
        first_bias,
        tables,
    )


def relative_onehot():
    offsets = jnp.arange(WS)[:, None] - jnp.arange(WS)[None, :] + WS - 1
    return (offsets[:, :, None] == jnp.arange(RELN)[None, None, :]).astype(jnp.float32)


def relative_tables(tables):
    onehot = relative_onehot()
    row_table = jnp.einsum("abr,rc->abc", onehot, tables[0], precision=precise)
    col_table = jnp.einsum("abr,rc->abc", onehot, tables[1], precision=precise)
    return (row_table, col_table)


def norm_parts(vector):
    centered = vector - jnp.mean(vector, axis=-1, keepdims=True)
    scale_inv = lax.rsqrt(jnp.mean(centered * centered, axis=-1, keepdims=True) + 1e-06)
    return (centered * scale_inv, scale_inv)


def norm_back(grad_normed, normed, scale_inv):
    return scale_inv * (
        grad_normed
        - jnp.mean(grad_normed, axis=-1, keepdims=True)
        - normed * jnp.mean(grad_normed * normed, axis=-1, keepdims=True)
    )


def window_mask(first_window, window_count):
    window_index = first_window + jnp.arange(window_count, dtype=jnp.int32)
    grid_spot = window_index % (GRID * GRID)
    token_index = jnp.arange(TOKW, dtype=jnp.int32)
    inside_rows = (grid_spot // GRID)[:, None] * WS + (token_index // WS)[None, :] < SIDE
    inside_cols = (grid_spot % GRID)[:, None] * WS + (token_index % WS)[None, :] < SIDE
    return (inside_rows & inside_cols).astype(jnp.float32)[:, :, None]


def contract_rows(left_part, right_part):
    return lax.dot_general(
        left_part, right_part, (((0,), (0,)), ((), ())), preferred_element_type=jnp.float32
    )


def contract_cols(left_part, right_part):
    return lax.dot_general(
        left_part, right_part, (((1,), (1,)), ((), ())), preferred_element_type=jnp.float32
    )


def attention_scores(query_heads, key_heads, row_table, col_table):
    window_total = query_heads.shape[0]
    direct = jnp.einsum(
        "wtha,wsha->whts", query_heads, key_heads, preferred_element_type=jnp.float32
    ) * HD ** (-0.5)
    query_grid = query_heads.reshape(window_total, WS, WS, HEADS, HD)
    along_rows = jnp.einsum(
        "wijhc,ikc->whijk",
        query_grid,
        row_table.astype(jnp.bfloat16),
        preferred_element_type=jnp.float32,
    )
    along_cols = jnp.einsum(
        "wijhc,jkc->whijk",
        query_grid,
        col_table.astype(jnp.bfloat16),
        preferred_element_type=jnp.float32,
    )
    relative = (along_rows[:, :, :, :, :, None] + along_cols[:, :, :, :, None, :]).reshape(
        window_total, HEADS, TOKW, TOKW
    )
    return direct + relative


def project(inputs, token_mask, w_qkv, vectors):
    window_total = inputs.shape[0]
    normed, scale_inv = norm_parts(inputs)
    first_normed = (
        ((normed * vectors[0] + vectors[2]) * token_mask)
        .astype(jnp.bfloat16)
        .reshape(window_total * TOKW, D)
    )
    bias_all = jnp.concatenate([vectors[4], jnp.zeros((D,), jnp.float32), vectors[5]])
    projected = jnp.dot(first_normed, w_qkv, preferred_element_type=jnp.float32) + bias_all

    def heads_of(block_part):
        return block_part.astype(jnp.bfloat16).reshape(window_total, TOKW, HEADS, HD)

    return (
        normed,
        scale_inv,
        first_normed,
        heads_of(projected[:, :D]),
        heads_of(projected[:, D : 2 * D]),
        heads_of(projected[:, 2 * D :]),
    )


def attend_forward(inputs_low, token_mask, w_qkv, w_proj, vectors, row_table, col_table):
    inputs = inputs_low.astype(jnp.float32)
    window_total = inputs.shape[0]
    normed, scale_inv, first_normed, query_heads, key_heads, value_heads = project(
        inputs, token_mask, w_qkv, vectors
    )
    scores = attention_scores(query_heads, key_heads, row_table, col_table)
    row_peak = jnp.max(scores, axis=-1, keepdims=True)
    log_total = row_peak + jnp.log(jnp.sum(jnp.exp(scores - row_peak), axis=-1, keepdims=True))
    attn_probs = jnp.exp(scores - log_total).astype(jnp.bfloat16)
    context = jnp.einsum(
        "whts,wsha->wtha", attn_probs, value_heads, preferred_element_type=jnp.float32
    )
    context = context.reshape(window_total * TOKW, D).astype(jnp.bfloat16)
    branch = jnp.dot(context, w_proj, preferred_element_type=jnp.float32) + vectors[6]
    middle = token_mask * (inputs + branch.reshape(window_total, TOKW, D))
    return (middle, (log_total, context))


def attend_backward(
    inputs_low, token_mask, grad_middle, w_qkv, w_proj, vectors, row_table, col_table, kept
):
    log_total, context = kept
    inputs = inputs_low.astype(jnp.float32)
    window_total = inputs.shape[0]
    normed, scale_inv, first_normed, query_heads, key_heads, value_heads = project(
        inputs, token_mask, w_qkv, vectors
    )
    scores = attention_scores(query_heads, key_heads, row_table, col_table)
    attn_probs = jnp.exp(scores - log_total)
    grad_branch = (token_mask * grad_middle).reshape(window_total * TOKW, D).astype(jnp.bfloat16)
    grad_proj = contract_rows(context, grad_branch)
    grad_proj_bias = jnp.sum(grad_branch.astype(jnp.float32), axis=0)
    grad_context = (
        contract_cols(grad_branch, w_proj)
        .astype(jnp.bfloat16)
        .reshape(window_total, TOKW, HEADS, HD)
    )
    grad_probs = jnp.einsum(
        "wtha,wsha->whts", grad_context, value_heads, preferred_element_type=jnp.float32
    )
    grad_values = jnp.einsum(
        "whts,wtha->wsha",
        attn_probs.astype(jnp.bfloat16),
        grad_context,
        preferred_element_type=jnp.float32,
    )
    grad_scores = (
        attn_probs * (grad_probs - jnp.sum(attn_probs * grad_probs, axis=-1, keepdims=True))
    ).astype(jnp.bfloat16)
    score_scale = HD ** (-0.5)
    grad_query = (
        jnp.einsum("whts,wsha->wtha", grad_scores, key_heads, preferred_element_type=jnp.float32)
        * score_scale
    )
    grad_keys = (
        jnp.einsum("whts,wtha->wsha", grad_scores, query_heads, preferred_element_type=jnp.float32)
        * score_scale
    )
    split_grad = grad_scores.astype(jnp.float32).reshape(window_total, HEADS, WS, WS, WS, WS)
    along_rows = jnp.sum(split_grad, axis=5)
    along_cols = jnp.sum(split_grad, axis=4)
    relative_query = jnp.einsum(
        "whijk,ikc->wijhc", along_rows, row_table, precision=precise
    ) + jnp.einsum("whijk,jkc->wijhc", along_cols, col_table, precision=precise)
    grad_query = grad_query + relative_query.reshape(window_total, TOKW, HEADS, HD)
    query_grid = query_heads.astype(jnp.float32).reshape(window_total, WS, WS, HEADS, HD)
    onehot = relative_onehot()
    grad_row_table = jnp.einsum("whijk,wijhc->ikc", along_rows, query_grid, precision=precise)
    grad_col_table = jnp.einsum("whijk,wijhc->jkc", along_cols, query_grid, precision=precise)
    grad_tables = jnp.stack(
        [
            jnp.einsum("abr,abc->rc", onehot, grad_row_table, precision=precise),
            jnp.einsum("abr,abc->rc", onehot, grad_col_table, precision=precise),
        ]
    )
    grad_projected = jnp.concatenate(
        [grad_query.reshape(-1, D), grad_keys.reshape(-1, D), grad_values.reshape(-1, D)], axis=1
    ).astype(jnp.bfloat16)
    grad_qkv = contract_rows(first_normed, grad_projected)
    column_sums = jnp.sum(grad_projected.astype(jnp.float32), axis=0)
    grad_first = contract_cols(grad_projected, w_qkv).reshape(window_total, TOKW, D) * token_mask
    grad_gain_one = jnp.sum(grad_first * normed, axis=(0, 1))
    grad_shift_one = jnp.sum(grad_first, axis=(0, 1))
    grad_inputs = token_mask * grad_middle + norm_back(grad_first * vectors[0], normed, scale_inv)
    return (
        grad_inputs,
        grad_qkv,
        grad_proj,
        (
            grad_gain_one,
            grad_shift_one,
            column_sums[:D],
            column_sums[2 * D :],
            grad_proj_bias,
            grad_tables,
        ),
    )


def feed_forward(middle, token_mask, w_fc1, vectors):
    window_total = middle.shape[0]
    normed, scale_inv = norm_parts(middle)
    second = (
        ((normed * vectors[1] + vectors[3]) * token_mask)
        .astype(jnp.bfloat16)
        .reshape(window_total * TOKW, D)
    )
    hidden = jnp.dot(second, w_fc1, preferred_element_type=jnp.float32) + vectors[8]
    active = (0.5 * hidden * (1.0 + jax.scipy.special.erf(hidden * root_half))).astype(jnp.bfloat16)
    return (normed, scale_inv, second, hidden, active)


def feed_backward(token_mask, cotangent, w_fc1, w_fc2, vectors, saved):
    normed, scale_inv, second, hidden, active = saved
    window_total = cotangent.shape[0]
    grad_out = cotangent.astype(jnp.float32)
    grad_update = (token_mask * grad_out).reshape(window_total * TOKW, D).astype(jnp.bfloat16)
    grad_fc2 = contract_rows(active, grad_update)
    grad_second_bias = jnp.sum(grad_update.astype(jnp.float32), axis=0)
    grad_active = contract_cols(grad_update, w_fc2)
    gelu_slope = (
        0.5 * (1.0 + jax.scipy.special.erf(hidden * root_half))
        + hidden * jnp.exp(-0.5 * hidden * hidden) * inv_root_two_pi
    )
    grad_hidden = (grad_active * gelu_slope).astype(jnp.bfloat16)
    grad_fc1 = contract_rows(second, grad_hidden)
    grad_first_bias = jnp.sum(grad_hidden.astype(jnp.float32), axis=0)
    grad_second = contract_cols(grad_hidden, w_fc1).reshape(window_total, TOKW, D) * token_mask
    grad_gain_two = jnp.sum(grad_second * normed, axis=(0, 1))
    grad_shift_two = jnp.sum(grad_second, axis=(0, 1))
    grad_middle = token_mask * grad_out + norm_back(grad_second * vectors[1], normed, scale_inv)
    return (
        grad_middle,
        grad_fc1,
        grad_fc2,
        (grad_gain_two, grad_shift_two, grad_second_bias, grad_first_bias),
    )


def slots_to_even(local, prev_last, next_first, first_window, window_count, even_base, per_even):
    extended = jnp.concatenate([prev_last[None], local, next_first[None]], axis=0)
    picked = lax.dynamic_slice_in_dim(extended, even_base - first_window + 1, per_even, 0)
    from_next = first_window + window_count <= even_base + per_even - 1
    last_window = jnp.where(from_next, next_first, picked[per_even - 1])
    return jnp.concatenate([picked[: per_even - 1], last_window[None]], axis=0)


def even_to_slots(local, prev_last, next_first, first_window, window_count, even_base, slot_total):
    padding = jnp.zeros((slot_total,) + local.shape[1:], local.dtype)
    extended = jnp.concatenate([prev_last[None], local, next_first[None], padding], axis=0)
    picked = lax.dynamic_slice_in_dim(extended, first_window - even_base + 1, slot_total, 0)
    live_slots = jnp.arange(slot_total) < window_count
    return jnp.where(live_slots[:, None, None], picked, jnp.zeros_like(picked))


def add_counts(earlier, later):
    return earlier + later


def adam_step(parameter, gradient, moment, square, first_fix, second_fix):
    moment_next = 0.5 * moment + 0.5 * gradient
    square_next = 0.999 * square + 0.001 * gradient * gradient
    fresh_weight = parameter - learn_rate * (moment_next / first_fix) / (
        jnp.sqrt(square_next / second_fix) + 1e-08
    )
    return (moment_next, square_next, fresh_weight.astype(jnp.bfloat16))


def per_device(
    x_slots,
    counts,
    cotangent,
    w_qkv,
    w_proj,
    w_fc1,
    w_fc2,
    small_params,
    moment_qkv,
    moment_proj,
    moment_fc1,
    moment_fc2,
    moment_small,
    square_qkv,
    square_proj,
    square_fc1,
    square_fc2,
    square_small,
):
    slot_total = x_slots.shape[0]
    per_even = cotangent.shape[0]
    win_at = lax.axis_index("win")
    grp_at = lax.axis_index("grp")
    holder = win_at * lax.axis_size("grp") + grp_at
    even_base = holder * per_even
    first_window = entering(counts, ("win", "grp"), add_counts, jnp.zeros((1,), jnp.int32))[0]
    window_count = counts[0]
    live_slots = (jnp.arange(slot_total) < window_count).astype(jnp.float32)[:, None, None]
    mask_slots = window_mask(first_window, slot_total) * live_slots
    unpacked = unpack(small_params.astype(jnp.float32))
    vectors = unpacked[:9]
    row_table, col_table = relative_tables(unpacked[9])
    middle_slots, kept = attend_forward(
        x_slots, mask_slots, w_qkv, w_proj, vectors, row_table, col_table
    )
    saved = feed_forward(middle_slots, mask_slots, w_fc1, vectors)
    update = jnp.dot(saved[4], w_fc2, preferred_element_type=jnp.float32) + vectors[7]
    block_slots = (mask_slots * (middle_slots + update.reshape(slot_total, TOKW, D))).astype(
        jnp.bfloat16
    )
    first_pair = jnp.stack([block_slots[0], cotangent[0]])
    last_pair = jnp.stack(
        [
            lax.dynamic_index_in_dim(block_slots, window_count - 1, 0, keepdims=False),
            cotangent[per_even - 1],
        ]
    )
    bordered = padded(jnp.stack([first_pair, last_pair]), ((("win", "grp"), 0),), 1)
    block_out = slots_to_even(
        block_slots, bordered[0][0], bordered[3][0], first_window, window_count, even_base, per_even
    )
    cotangent_slots = even_to_slots(
        cotangent, bordered[0][1], bordered[3][1], first_window, window_count, even_base, slot_total
    )
    grad_middle, grad_fc1, grad_fc2, feed_small = feed_backward(
        mask_slots, cotangent_slots, w_fc1, w_fc2, vectors, saved
    )
    grad_inputs, grad_qkv, grad_proj, attend_small = attend_backward(
        x_slots, mask_slots, grad_middle, w_qkv, w_proj, vectors, row_table, col_table, kept
    )
    input_grad = grad_inputs.astype(jnp.bfloat16)
    grad_small_local = jnp.concatenate(
        [
            attend_small[0],
            feed_small[0],
            attend_small[1],
            feed_small[1],
            attend_small[2],
            attend_small[3],
            attend_small[4],
            feed_small[2],
            feed_small[3],
            attend_small[5].reshape(-1),
        ]
    )
    part_a, part_b, part_c, part_d = (
        lax.psum_scatter(grad_qkv, "win", scatter_dimension=0, tiled=True),
        lax.psum_scatter(grad_proj, "win", scatter_dimension=0, tiled=True),
        lax.psum_scatter(grad_fc1, "win", scatter_dimension=0, tiled=True),
        lax.psum_scatter(grad_fc2, "win", scatter_dimension=0, tiled=True),
    )
    part_a, part_b, part_c, part_d = (
        lax.psum_scatter(
            part_a.astype(jnp.bfloat16), "grp", scatter_dimension=1, tiled=True
        ).astype(jnp.float32),
        lax.psum_scatter(
            part_b.astype(jnp.bfloat16), "grp", scatter_dimension=1, tiled=True
        ).astype(jnp.float32),
        lax.psum_scatter(
            part_c.astype(jnp.bfloat16), "grp", scatter_dimension=1, tiled=True
        ).astype(jnp.float32),
        lax.psum_scatter(
            part_d.astype(jnp.bfloat16), "grp", scatter_dimension=1, tiled=True
        ).astype(jnp.float32),
    )
    grad_small = lax.psum(grad_small_local, ("win", "grp"))

    def owned_part(weight, piece):
        return lax.dynamic_slice(
            weight, (win_at * piece.shape[0], grp_at * piece.shape[1]), piece.shape
        ).astype(jnp.float32)

    step_value = jnp.float32(STEP)
    first_fix = 1.0 - jnp.power(jnp.float32(0.5), step_value)
    second_fix = 1.0 - jnp.power(jnp.float32(0.999), step_value)
    upd_qkv = adam_step(
        owned_part(w_qkv, part_a), part_a, moment_qkv, square_qkv, first_fix, second_fix
    )
    upd_proj = adam_step(
        owned_part(w_proj, part_b), part_b, moment_proj, square_proj, first_fix, second_fix
    )
    upd_fc1 = adam_step(
        owned_part(w_fc1, part_c), part_c, moment_fc1, square_fc1, first_fix, second_fix
    )
    upd_fc2 = adam_step(
        owned_part(w_fc2, part_d), part_d, moment_fc2, square_fc2, first_fix, second_fix
    )
    upd_small = adam_step(
        small_params.astype(jnp.float32),
        grad_small,
        moment_small,
        square_small,
        first_fix,
        second_fix,
    )
    new_qkv, new_proj, new_fc1, new_fc2 = (
        lax.all_gather(upd_qkv[2], "win", axis=0, tiled=True),
        lax.all_gather(upd_proj[2], "win", axis=0, tiled=True),
        lax.all_gather(upd_fc1[2], "win", axis=0, tiled=True),
        lax.all_gather(upd_fc2[2], "win", axis=0, tiled=True),
    )
    return (
        block_out,
        input_grad,
        part_a,
        part_b,
        part_c,
        part_d,
        grad_small,
        upd_qkv[0],
        upd_proj[0],
        upd_fc1[0],
        upd_fc2[0],
        upd_small[0],
        upd_qkv[1],
        upd_proj[1],
        upd_fc1[1],
        upd_fc2[1],
        upd_small[1],
        new_qkv,
        new_proj,
        new_fc1,
        new_fc2,
        upd_small[2],
    )


def solution(mesh):
    in_specs = (
        P(("win", "grp"), None, None),
        P(("win", "grp")),
        P(("win", "grp"), None, None),
        P(),
        P(),
        P(),
        P(),
        P(),
        P("win", "grp"),
        P("win", "grp"),
        P("win", "grp"),
        P("win", "grp"),
        P(),
        P("win", "grp"),
        P("win", "grp"),
        P("win", "grp"),
        P("win", "grp"),
        P(),
    )
    out_specs = (
        P(("win", "grp"), None, None),
        P(("win", "grp"), None, None),
        P("win", "grp"),
        P("win", "grp"),
        P("win", "grp"),
        P("win", "grp"),
        P(),
        P("win", "grp"),
        P("win", "grp"),
        P("win", "grp"),
        P("win", "grp"),
        P(),
        P("win", "grp"),
        P("win", "grp"),
        P("win", "grp"),
        P("win", "grp"),
        P(),
        P(None, "grp"),
        P(None, "grp"),
        P(None, "grp"),
        P(None, "grp"),
        P(),
    )
    return jax.shard_map(
        per_device, mesh=mesh, in_specs=in_specs, out_specs=out_specs, check_vma=False
    )
```

profile of v0, /device:TPU:0, one launch (start us, length us, event | category | flops | bytes accessed | tf_op | source)
XLA Modules:
  0.0 1112.0 jit_solution(2316188035389983951)
XLA Ops:
  11.7 42.0 %all-reduce = s32[32]{0:T(128)S(1)} all-reduce(s32[32]{0:T(128)S(1)} %dynamic-update-slice), channel_id=2, replica_groups=mesh['win'=8,'grp'=4] {'win','grp'}, use_global_device_ids=true, to_apply=%add | all-reduce | flops 32 | bytes 256
  60.2 6.2 add_convert_fusion
  83.0 5.0 copy.160
  88.1 6.7 copy.159
  94.7 5.8 reshape.415
  100.5 6.6 copy.165
  107.2 13.1 %fusion.41 = f32[5,12,14,14,14]{2,4,1,0,3:T(8,128)} fusion(bf16[5,14,14,12,64]{4,3,2,1,0:T(8,128)(2,1)} %reshape_reshape.4, f32[14,14,64]{2,1,0:T(8,128)S(1)} %fusion.65), kind=kOutput, calls=%fused_computation.74 | convolution fusion | flops 21086464 | bytes 2214016 | tf_op jit(solution)/shard_map/wijhc,jkc->whijk/dot_general | solution.py:132
  120.2 9.5 copy.164
  129.7 10.4 fusion.38
  143.6 30.1 %broadcast_add_fusion = f32[5,12,14,14,14,14]{3,2,5,4,1,0:T(8,128)} fusion(f32[5,12,14,14,14]{3,2,4,1,0:T(8,128)S(1)} %bitcast.144, f32[5,12,14,14,14]{3,2,4,1,0:T(8,128)S(1)} %copy.162), kind=kLoop, calls=%fused_computation.1 | loop fusion | flops 2304960 | bytes 10536960 | tf_op jit(solution)/shard_map/add | solution.py:138
  173.7 55.4 %add.417 = f32[5,12,196,196]{2,3,1,0:T(8,128)} reshape(f32[5,12,14,14,14,14]{3,2,5,4,1,0:T(8,128)} %broadcast_add_fusion) | data formatting | bytes 18439680 | tf_op jit(solution)/shard_map/add | solution.py:138
  229.1 7.4 fusion.103
  262.3 10.4 multiply_convert_fusion.1
  275.3 8.8 convolution_add_fusion.1
  315.1 9.8 fusion.107
  325.0 12.6 %convert_reduce_fusion = (f32[3072]{0:T(1024)}, bf16[980,3072]{1,0:T(8,128)(2,1)S(1)}) fusion(f32[980,3072]{1,0:T(8,128)} %get-tuple-element.198, f32[3072]{0:T(1024)S(1)} %copy-done.69, bf16[980,768]{1,0:T(8,128)(2,1)} %convert_element_type.174, bf16[3072,768]{1,0:T(8,128)(2,1)} %param.26), kind=kOutput, calls=%fused_computation.14 | convolution fusion | flops 4663354368 | bytes 24311808 | tf_op jit(solution)/shard_map/dot_general | solution.py:115
  340.1 7.6 fusion.106
  349.1 11.4 %multiply_reduce_fusion.7 = (f32[768]{0:T(1024)}, f32[980]{0:T(1024)S(1)}, f32[980,768]{1,0:T(8,128)}) fusion(f32[980]{0:T(1024)S(1)} %fusion.80, f32[768]{0:T(1024)S(1)} %get-tuple-element.186, bf16[980,3072]{1,0:T(8,128)(2,1)} %copy-done.82, bf16[768,3072]{1,0:T(8,128)(2,1)} %param.25), kind=kOutput, calls=%fused_computation.72 | convolution fusion | flops 4627228672 | bytes 13764256 | tf_op jit(solution)/shard_map/dot_general | solution.py:115
  377.1 4.4 reshape.418
  381.5 6.2 copy.175
  387.7 8.3 multiply_reduce_fusion
  396.0 9.4 multiply_convert_fusion
  405.4 53.5 %reshape.393 = f32[5,12,14,14,14,14]{3,2,5,4,1,0:T(8,128)} reshape(bf16[5,12,196,196]{2,3,1,0:T(8,128)(2,1)} %multiply_convert_fusion) | data formatting | bytes 13829760 | tf_op jit(solution)/shard_map/reshape | solution.py:227
  461.9 36.5 %fusion.87 = (f32[5,12,14,14,14]{3,2,4,1,0:T(8,128)}, f32[5,12,14,14,14]{3,2,4,1,0:T(8,128)}) fusion(f32[5,12,14,14,14,14]{3,2,5,4,1,0:T(8,128)} %reshape.393), kind=kLoop, calls=%fused_computation.188 | loop fusion | flops 4280640 | bytes 10536960 | tf_op jit(solution)/shard_map/reduce_sum | solution.py:228
  498.4 6.6 convert_bitcast_fusion
  508.1 5.7 reshape.389
  513.8 4.8 fusion.44
  523.6 11.0 copy.180
  534.6 8.5 fusion.62
  543.2 15.8 %bitcast_add_fusion = f32[5,14,14,12,64]{4,2,3,0,1:T(8,128)S(1)} fusion(f32[14,64,5,12,14]{1,4,3,2,0:T(8,128)S(1)} %fusion.62, f32[5,12,14,14,14]{3,2,4,1,0:T(8,128)S(1)} %bitcast.142, f32[14,14,64]{2,1,0:T(8,128)S(1)} %copy-done.33), kind=kOutput, calls=%fused_computation.20 | convolution fusion | flops 127196160 | bytes 6729856 | tf_op jit(solution)/shard_map/whijk,ikc->wijhc/dot_general | solution.py:230
  562.6 7.1 reshape.386
  569.7 6.5 copy.183
  576.2 5.4 fusion.13
  591.3 6.0 fusion.104
  600.2 7.6 multiply_reduce_fusion.6
  615.8 11.5 %copy.191 = f32[5,12,14,14,14]{1,4,0,3,2:T(8,128)} copy(f32[5,12,14,14,14]{3,2,4,1,0:T(8,128)} %get-tuple-element.134) | data formatting | bytes 1317120 | tf_op jit(solution)/shard_map/reduce_sum | solution.py:228
  627.4 12.1 %copy.193 = f32[5,12,14,14,14]{1,4,0,2,3:T(8,128)} copy(f32[5,12,14,14,14]{3,2,4,1,0:T(8,128)} %get-tuple-element.135) | data formatting | bytes 1317120 | tf_op jit(solution)/shard_map/reduce_sum | solution.py:229
  639.6 12.2 %fusion.51 = f32[14,14,64]{2,1,0:T(8,128)S(1)} fusion(f32[5,12,14,14,14]{1,4,0,3,2:T(8,128)} %copy.191, bf16[5,14,14,12,64]{4,3,2,1,0:T(8,128)(2,1)} %reshape_reshape.4), kind=kOutput, calls=%fused_computation.88 | convolution fusion | flops 126443520 | bytes 2214016 | tf_op jit(solution)/shard_map/whijk,wijhc->ikc/dot_general | solution.py:236
  652.2 50.1 %reduce-scatter.19.cloned.1.call-done = f32[96,3072]{1,0:T(8,128)} async-done(((f32[768,3072]{1,0:T(8,128)}), f32[96,3072]{1,0:T(8,128)}) %reduce-scatter.19.cloned.1.call-update) | async-done | bytes 1179664 | tf_op jit(solution)/shard_map/reduce_scatter | solution.py:416
  705.0 12.2 %fusion.54 = f32[14,14,64]{2,1,0:T(8,128)S(1)} fusion(f32[5,12,14,14,14]{1,4,0,2,3:T(8,128)} %copy.193, bf16[5,14,14,12,64]{4,3,2,1,0:T(8,128)(2,1)} %reshape_reshape.4), kind=kOutput, calls=%fused_computation.89 | convolution fusion | flops 126443520 | bytes 2214016 | tf_op jit(solution)/shard_map/whijk,wijhc->jkc/dot_general | solution.py:237
  718.0 55.9 %reduce-scatter.17.cloned.1.call-done = f32[96,768]{1,0:T(8,128)} async-done(((f32[768,768]{1,0:T(8,128)}), f32[96,768]{1,0:T(8,128)}) %reduce-scatter.17.cloned.1.call-update) | async-done | bytes 294928 | tf_op jit(solution)/shard_map/reduce_scatter | solution.py:415
  778.9 126.7 %reduce-scatter.15.cloned.1.call-done = f32[96,2304]{1,0:T(8,128)} async-done(((f32[768,2304]{1,0:T(8,128)}), f32[96,2304]{1,0:T(8,128)}) %reduce-scatter.15.cloned.1.call-update) | async-done | bytes 884752 | tf_op jit(solution)/shard_map/reduce_scatter | solution.py:414
  909.0 20.2 %reduce-scatter.29.cloned.1.call-done = bf16[192,384]{1,0:T(8,128)(2,1)} async-done(((bf16[768,384]{1,0:T(8,128)(2,1)}), bf16[192,384]{1,0:T(8,128)(2,1)}) %reduce-scatter.29.cloned.1.call-update) | async-done | bytes 147472
  932.9 40.0 %psum.7 = f32[12672]{0:T(1024)S(1)} all-reduce(f32[12672]{0:T(1024)S(1)} %constant_dynamic-update-slice_fusion.6), channel_id=1, replica_groups=mesh['win'=8,'grp'=4] {'win','grp'}, use_global_device_ids=true, to_apply=%region_31.32 | all-reduce | flops 12672 | bytes 101376 | tf_op jit(solution)/shard_map/psum | solution.py:433
  976.5 6.1 fusion.31
  989.0 31.3 %all_gather.21 = bf16[768,192]{1,0:T(8,128)(2,1)S(1)} all-gather(bf16[96,192]{1,0:T(8,128)(2,1)S(1)} %get-tuple-element.157), channel_id=1, replica_groups=mesh['win'=8,'grp'=4] {'win'}, dimensions={0}, use_global_device_ids=true | all-gather | bytes 331776 | tf_op jit(solution)/shard_map/all_gather | solution.py:465
  1024.8 35.4 %all_gather.20 = bf16[768,576]{1,0:T(8,128)(2,1)S(1)} all-gather(bf16[96,576]{1,0:T(8,128)(2,1)S(1)} %get-tuple-element.160), channel_id=1, replica_groups=mesh['win'=8,'grp'=4] {'win'}, dimensions={0}, use_global_device_ids=true | all-gather | bytes 995328 | tf_op jit(solution)/shard_map/all_gather | solution.py:464
  1068.0 34.6 %all-gather.4.cloned.1.call-done = bf16[768,768]{1,0:T(8,128)(2,1)} async-done(((bf16[96,768]{1,0:T(8,128)(2,1)}), bf16[768,768]{1,0:T(8,128)(2,1)}) %all-gather.4.cloned.1.call-update) | async-done | bytes 1179664 | tf_op jit(solution)/shard_map/all_gather | solution.py:466
  (346 shorter events, 185.4 us)
Async XLA Ops:
  7.2 50.8 %copy-start.3 = (bf16[5,196,768]{2,1,0:T(8,128)(2,1)S(1)}, bf16[5,196,768]{2,1,0:T(8,128)(2,1)}, u32[]{:S(2)}) copy-start(bf16[5,196,768]{2,1,0:T(8,128)(2,1)} %param.20) | copy-start | bytes 4515844
  7.2 602.8 %reduce-scatter.23.cloned.1.call-start = ((), (), s32[]{:S(2)}) async-start(), calls=%async_computation.12 | async-start | bytes 10616832 | tf_op jit(solution)/shard_map/reduce_scatter | solution.py:417
  7.3 51.5 %copy-start.70 = (s32[196]{0:T(256)}, s32[196]{0:T(256)S(1)}, u32[]{:S(2)}) copy-start(s32[196]{0:T(256)S(1)} %get-tuple-element.207) | copy-start | bytes 2356
  7.3 51.5 %copy-start.72 = (s32[196]{0:T(256)}, s32[196]{0:T(256)S(1)}, u32[]{:S(2)}) copy-start(s32[196]{0:T(256)S(1)} %get-tuple-element.208) | copy-start | bytes 2356
  7.3 69.3 %copy-start.49 = (s32[14,14]{1,0:T(8,128)}, s32[14,14]{1,0:T(8,128)S(1)}, u32[]{:S(2)}) copy-start(s32[14,14]{1,0:T(8,128)S(1)} %subtract_add_fusion) | copy-start | bytes 2356
  10.9 47.9 %copy-start.63 = (f32[768]{0:T(1024)}, f32[768]{0:T(1024)S(1)}, u32[]{:S(2)}) copy-start(f32[768]{0:T(1024)S(1)} %get-tuple-element.191) | copy-start | bytes 9220
  10.9 357.5 %copy-start.57 = (f32[768]{0:T(1024)}, f32[768]{0:T(1024)S(1)}, u32[]{:S(2)}) copy-start(f32[768]{0:T(1024)S(1)} %get-tuple-element.186) | copy-start | bytes 9220
  58.0 310.3 %copy-start.38 = (f32[5,196]{1,0:T(8,128)}, f32[5,196]{1,0:T(8,128)S(1)}, u32[]{:S(2)}) copy-start(f32[5,196]{1,0:T(8,128)S(1)} %fusion.78) | copy-start | bytes 11764
  76.7 30.5 %copy-start.34 = (f32[14,14,64]{2,1,0:T(8,128)}, f32[14,14,64]{2,1,0:T(8,128)S(1)}, u32[]{:S(2)}) copy-start(f32[14,14,64]{2,1,0:T(8,128)S(1)} %fusion.65) | copy-start | bytes 150532
  76.9 52.8 %copy-start.32 = (f32[14,14,64]{2,1,0:T(8,128)}, f32[14,14,64]{2,1,0:T(8,128)S(1)}, u32[]{:S(2)}) copy-start(f32[14,14,64]{2,1,0:T(8,128)S(1)} %fusion.66) | copy-start | bytes 150532
  88.0 141.0 %copy-start.7 = (bf16[5,196,12,64]{1,3,2,0:T(8,128)(2,1)}, bf16[5,196,12,64]{1,3,2,0:T(8,128)(2,1)S(1)}, u32[]{:S(2)}) copy-start(bf16[5,196,12,64]{1,3,2,0:T(8,128)(2,1)S(1)} %copy.160) | copy-start | bytes 4515844
  256.8 111.6 %copy-start.1 = (f32[5,196,768]{2,1,0:T(8,128)}, f32[5,196,768]{2,1,0:T(8,128)S(1)}, u32[]{:S(2)}) copy-start(f32[5,196,768]{2,1,0:T(8,128)S(1)} %get-tuple-element.169) | copy-start | bytes 9031684
  256.8 111.6 %copy-start.44 = (f32[5,196]{1,0:T(8,128)}, f32[5,196]{1,0:T(8,128)S(1)}, u32[]{:S(2)}) copy-start(f32[5,196]{1,0:T(8,128)S(1)} %broadcast_multiply_fusion.7) | copy-start | bytes 11764
  257.3 111.1 %copy-start.53 = (f32[5,196]{1,0:T(8,128)}, f32[5,196]{1,0:T(8,128)S(1)}, u32[]{:S(2)}) copy-start(f32[5,196]{1,0:T(8,128)S(1)} %add_rsqrt_fusion) | copy-start | bytes 11764
  294.7 6.5 collective-permute-start.1
  297.4 7.1 collective-permute-start
  325.0 377.4 %reduce-scatter.19.cloned.1.call-start = ((), (), s32[]{:S(2)}) async-start(), calls=%async_computation.10 | async-start | bytes 10616832 | tf_op jit(solution)/shard_map/reduce_scatter | solution.py:416
  347.8 426.1 %reduce-scatter.17.cloned.1.call-start = ((), (), s32[]{:S(2)}) async-start(), calls=%async_computation.9 | async-start | bytes 2654208 | tf_op jit(solution)/shard_map/reduce_scatter | solution.py:415
  405.4 53.5 %copy-start.22 = (bf16[980,768]{0,1:T(8,128)(2,1)S(1)}, bf16[980,768]{0,1:T(8,128)(2,1)}, u32[]{:S(2)}) copy-start(bf16[980,768]{0,1:T(8,128)(2,1)} %convert_element_type.168) | copy-start | bytes 4515844
  405.4 53.5 %copy-start.29 = (bf16[980,768]{1,0:T(8,128)(2,1)S(1)}, bf16[980,768]{1,0:T(8,128)(2,1)}, u32[]{:S(2)}) copy-start(bf16[980,768]{1,0:T(8,128)(2,1)} %copy-done.28) | copy-start | bytes 4515844
  461.8 36.6 %copy-start.12 = (bf16[5,196,12,64]{1,3,2,0:T(8,128)(2,1)S(1)}, bf16[5,196,12,64]{1,3,2,0:T(8,128)(2,1)}, u32[]{:S(2)}) copy-start(bf16[5,196,12,64]{1,3,2,0:T(8,128)(2,1)} %copy.175) | copy-start | bytes 4515844
  461.8 443.7 %reduce-scatter.15.cloned.1.call-start = ((), (), s32[]{:S(2)}) async-start(), calls=%async_computation.8 | async-start | bytes 7962624 | tf_op jit(solution)/shard_map/reduce_scatter | solution.py:414
  523.6 19.5 %slice-start = ((s8[6881280]{0:T(1024)(128)(4,1)}), s8[2686976]{0:T(1024)(128)(4,1)S(1)}, s32[]{:S(2)}) async-start(s8[6881280]{0:T(1024)(128)(4,1)} %bitcast.141), calls=%async_computation.18 | async-start | bytes 5373952
  597.4 331.8 %reduce-scatter.29.cloned.1.call-start = ((), (), s32[]{:S(2)}) async-start(), calls=%async_computation.17 | async-start | bytes 737280
  612.6 370.0 %reduce-scatter.21.cloned.1.call-start = ((), (), s32[]{:S(2)}) async-start(), calls=%async_computation.11 | async-start | bytes 737280 | tf_op jit(solution)/shard_map/reduce_scatter | solution.py:426
  704.5 281.9 %reduce-scatter.27.cloned.1.call-start = ((), (), s32[]{:S(2)}) async-start(), calls=%async_computation.16 | async-start | bytes 245760
  717.9 190.0 %copy-start.19 = (bf16[3,196,768]{2,1,0:T(8,128)(2,1)}, bf16[3,196,768]{2,1,0:T(8,128)(2,1)S(1)}, u32[]{:S(2)}) copy-start(bf16[3,196,768]{2,1,0:T(8,128)(2,1)S(1)} %fusion.58) | copy-start | bytes 2709508
  775.7 132.2 %copy-start.74 = (f32[768]{0:T(1024)S(1)}, f32[768]{0:T(1024)}, u32[]{:S(2)}) copy-start(f32[768]{0:T(1024)} %get-tuple-element.140) | copy-start | bytes 9220
  775.7 246.1 %reduce-scatter.25.cloned.1.call-start = ((), (), s32[]{:S(2)}) async-start(), calls=%async_computation.15 | async-start | bytes 737280
  778.9 130.1 %copy-start.65 = (f32[768]{0:T(1024)S(1)}, f32[768]{0:T(1024)}, u32[]{:S(2)}) copy-start(f32[768]{0:T(1024)} %get-tuple-element.166) | copy-start | bytes 9220
  906.7 26.1 %copy-start.67 = (f32[768]{0:T(1024)S(1)}, f32[768]{0:T(1024)}, u32[]{:S(2)}) copy-start(f32[768]{0:T(1024)} %get-tuple-element.163) | copy-start | bytes 9220
  906.8 26.2 %copy-start.68 = (f32[3072]{0:T(1024)S(1)}, f32[3072]{0:T(1024)}, u32[]{:S(2)}) copy-start(f32[3072]{0:T(1024)} %get-tuple-element.203) | copy-start | bytes 36868
  907.8 157.7 %all-gather.6.cloned.1.call-start = ((), (), s32[]{:S(2)}) async-start(), calls=%async_computation.14 | async-start | bytes 1769472 | tf_op jit(solution)/shard_map/all_gather | solution.py:467
  908.8 67.6 %copy-start.2 = (f32[5,196,768]{2,1,0:T(8,128)S(1)}, f32[5,196,768]{2,1,0:T(8,128)}, u32[]{:S(2)}) copy-start(f32[5,196,768]{2,1,0:T(8,128)} %copy-done.1) | copy-start | bytes 9031684
  908.8 67.6 %copy-start.45 = (f32[5,196]{1,0:T(8,128)S(1)}, f32[5,196]{1,0:T(8,128)}, u32[]{:S(2)}) copy-start(f32[5,196]{1,0:T(8,128)} %copy-done.44) | copy-start | bytes 11764
  908.8 67.6 %copy-start.54 = (f32[5,196]{1,0:T(8,128)S(1)}, f32[5,196]{1,0:T(8,128)}, u32[]{:S(2)}) copy-start(f32[5,196]{1,0:T(8,128)} %copy-done.53) | copy-start | bytes 11764
  908.8 67.6 %copy-start.58 = (f32[768]{0:T(1024)S(1)}, f32[768]{0:T(1024)}, u32[]{:S(2)}) copy-start(f32[768]{0:T(1024)} %copy-done.57) | copy-start | bytes 9220
  908.8 67.6 %copy-start.60 = (f32[5,196]{1,0:T(8,128)S(1)}, f32[5,196]{1,0:T(8,128)}, u32[]{:S(2)}) copy-start(f32[5,196]{1,0:T(8,128)} %copy-done.59) | copy-start | bytes 11764
  908.8 67.6 %copy-start.62 = (f32[5,196]{1,0:T(8,128)S(1)}, f32[5,196]{1,0:T(8,128)}, u32[]{:S(2)}) copy-start(f32[5,196]{1,0:T(8,128)} %copy-done.61) | copy-start | bytes 11764
  932.8 169.7 %all-gather.4.cloned.1.call-start = ((), (), s32[]{:S(2)}) async-start(), calls=%async_computation.13 | async-start | bytes 1327104 | tf_op jit(solution)/shard_map/all_gather | solution.py:466
  982.6 40.3 %copy-start.36 = (f32[96,576]{1,0:T(8,128)S(1)}, f32[96,576]{1,0:T(8,128)}, u32[]{:S(2)}) copy-start(f32[96,576]{1,0:T(8,128)} %param.28) | copy-start | bytes 663556
  982.6 40.3 %copy-start.46 = (f32[96,576]{1,0:T(8,128)S(1)}, f32[96,576]{1,0:T(8,128)}, u32[]{:S(2)}) copy-start(f32[96,576]{1,0:T(8,128)} %param.33) | copy-start | bytes 663556
  984.8 80.0 %copy-start.31 = (f32[96,768]{1,0:T(8,128)}, f32[96,768]{1,0:T(8,128)S(1)}, u32[]{:S(2)}) copy-start(f32[96,768]{1,0:T(8,128)S(1)} %get-tuple-element.284) | copy-start | bytes 884740
  989.0 73.2 %copy-start.41 = (f32[96,192]{1,0:T(8,128)}, f32[96,192]{1,0:T(8,128)S(1)}, u32[]{:S(2)}) copy-start(f32[96,192]{1,0:T(8,128)S(1)} %get-tuple-element.283) | copy-start | bytes 221188
  1021.2 41.8 %copy-start.24 = (f32[384,192]{1,0:T(8,128)S(1)}, f32[384,192]{1,0:T(8,128)}, u32[]{:S(2)}) copy-start(f32[384,192]{1,0:T(8,128)} %get-tuple-element.182) | copy-start | bytes 884740
  1022.9 41.0 %copy-start.23 = (f32[384,192]{1,0:T(8,128)S(1)}, f32[384,192]{1,0:T(8,128)}, u32[]{:S(2)}) copy-start(f32[384,192]{1,0:T(8,128)} %get-tuple-element.183) | copy-start | bytes 884740
  1024.8 40.7 %copy-start.37 = (f32[96,576]{1,0:T(8,128)}, f32[96,576]{1,0:T(8,128)S(1)}, u32[]{:S(2)}) copy-start(f32[96,576]{1,0:T(8,128)S(1)} %get-tuple-element.282) | copy-start | bytes 663556
  1024.8 40.0 %copy-start.30 = (f32[96,768]{1,0:T(8,128)S(1)}, f32[96,768]{1,0:T(8,128)}, u32[]{:S(2)}) copy-start(f32[96,768]{1,0:T(8,128)} %param.30) | copy-start | bytes 884740
  (52 other events, 274.2 us)
Sparse Core Ops, SparseCore 0:
  325.1 210.9 reduce-scatter.22
  539.7 162.5 reduce-scatter.18
  705.8 68.0 reduce-scatter.16
  777.4 128.0 reduce-scatter.14
  908.0 21.1 reduce-scatter.28
  931.7 22.0 reduce-scatter.20
  956.9 19.7 reduce-scatter.26
  979.9 22.0 reduce-scatter.24
  1004.5 54.7 all-gather.5
  1061.5 41.0 all-gather.3
where the time goes:
time: 1120 us; the launch traced here: 1110 us
  local copies, waits for them, and re-layouts  317 us (28%)
  waiting for transfers between devices  288 us (26%)
  matrix products  198 us (18%)
  blocking collectives  149 us (13%)
  other arithmetic  139 us (12%)
  between operations  16.3 us (1%)
    reduce_scatter x1, waiting for transfers between devices, per_device(): lax.psum_scatter(grad_qkv, 'win', scatter_dimension=0, tiled=True)  127 us
    reduce_scatter x1, waiting for transfers between devices, per_device(): lax.psum_scatter(grad_proj, 'win', scatter_dimension=0, tiled=True)  55.9 us
    add x1, local copies, waits for them, and re-layouts, attention_scores(): along_rows[:, :, :, :, :, None] + along_cols[:, :, :, :, None, :]  55.4 us
    reshape x1, local copies, waits for them, and re-layouts, attend_backward(): grad_scores.astype(jnp.float32).reshape(window_total, HEADS, WS, WS, WS, WS)  53.5 us
    reduce_scatter x1, waiting for transfers between devices, per_device(): lax.psum_scatter(grad_fc1, 'win', scatter_dimension=0, tiled=True)  50.1 us
    unnamed x1, blocking collectives  42 us
    psum x1, blocking collectives, per_device(): grad_small = lax.psum(grad_small_local, ('win', 'grp'))  40 us
    reduce_sum x1, other arithmetic, attend_backward(): along_rows = jnp.sum(split_grad, axis=5)  36.5 us
  transfers between devices with their start and end apart: 12, of which 5 were waited for; matrix products, arithmetic and copies ran while one was open for 34% of the time, Pallas kernels for 0%

commit v1 on v0

v1 whole, which is shorter than its diff:
```python
import functools

import jax
import jax.numpy as jnp
from jax import lax
from jax.experimental import pallas as pl
from jax.experimental.pallas import tpu as pltpu
from jax.sharding import PartitionSpec as P

D = 768
HEADS = 12
HD = 64
FF = 3072
WS = 14
SIDE = 64
STEP = 4
TOKW = 196
GRID = 5
RELN = 27
TP = 224

root_half = 0.7071067811865476
inv_root_two_pi = 0.3989422804014327
learn_rate = 0.06
bf16 = jnp.bfloat16
f32 = jnp.float32
VMEM_LIMIT = 56 << 20


def dot(a, b):
    return lax.dot_general(a, b, (((1,), (0,)), ((), ())), preferred_element_type=f32)


def dot_nt(a, b):
    return lax.dot_general(a, b, (((1,), (1,)), ((), ())), preferred_element_type=f32)


def dot_tn(a, b):
    return lax.dot_general(a, b, (((0,), (0,)), ((), ())), preferred_element_type=f32)


def iota(shape, axis):
    return lax.broadcasted_iota(jnp.int32, shape, axis)


def spread():
    row, token = iota((TP, TOKW), 0), iota((TP, TOKW), 1)
    hit = ((row & 15) < WS) & (token == WS * (row >> 4) + (row & 15))
    return hit.astype(f32).astype(bf16)


def gather_rows():
    token, row = iota((TOKW, TP), 0), iota((TOKW, TP), 1)
    hit = ((row & 15) < WS) & (token == WS * (row >> 4) + (row & 15))
    return hit.astype(f32).astype(bf16)


def key_lanes():
    row, lane = iota((TP, 128), 0), iota((TP, 128), 1)
    i, j = row >> 4, row & 15
    low = lane & 31
    hit = (low < WS) & (((lane < 64) & (low == i)) | ((lane >= 64) & (low == j)))
    shut = (lane == 127) & (j >= WS)
    return jnp.where(shut, -1e30, hit.astype(f32)).astype(bf16)


def inside(limit_row, limit_col):
    row = iota((TP, 1), 0)
    i, j = row >> 4, row & 15
    return ((i < limit_row) & (j < jnp.minimum(limit_col, WS))).astype(f32)


def norm_parts(v):
    centered = v - jnp.mean(v, axis=-1, keepdims=True)
    scale_inv = lax.rsqrt(jnp.mean(centered * centered, axis=-1, keepdims=True) + 1e-06)
    return centered * scale_inv, scale_inv


def norm_back(e, normed, scale_inv):
    return scale_inv * (
        e
        - jnp.mean(e, axis=-1, keepdims=True)
        - normed * jnp.mean(e * normed, axis=-1, keepdims=True)
    )


def lane_mask(head):
    lane = iota((1, 128), 1)
    return ((lane < HD) if head == 0 else (lane >= HD)).astype(f32).astype(bf16)


def query_rolls(table):
    lane = iota((16, 128), 1)
    out = []
    for i in range(WS):
        tile = table[16 * i : 16 * i + 16]
        by_row = pltpu.roll(tile, 51 + i, 1)
        by_col = pltpu.roll(tile, 51, 1, stride=1, stride_axis=0)
        kept = jnp.where(lane < WS, by_row, 0.0)
        out.append(jnp.where((lane >= 64) & (lane < 64 + WS), by_col, kept))
    return jnp.concatenate(out, axis=0)


def query_lanes(table):
    aug = query_rolls(table)
    high = aug.astype(bf16).astype(f32)
    full = high + pltpu.roll(aug - high, 32, 1)
    return jnp.where(iota((TP, 128), 1) == 127, 1.0, full).astype(bf16)


def fwd_kernel(
    info, xs_ref, prev_ref, next_ref, wqkv_ref, wproj_ref, vec_ref, bias_ref, tab_ref,
    xpad_ref, n1_ref, qkv_ref, pt_ref, o_ref, h_ref, n2_ref,
):
    k = pl.program_id(0)
    source = info[k, 1]
    x = jnp.where(source == 0, xs_ref[0], jnp.where(source == 1, prev_ref[0], next_ref[0]))
    big = dot(spread(), x)
    xpad_ref[0] = big.astype(bf16)
    mask = inside(info[k, 2], info[k, 3])
    vec = vec_ref[...]
    normed, _ = norm_parts(big)
    n1 = (mask * (normed * vec[0:1] + vec[2:3])).astype(bf16)
    n1_ref[0] = n1
    qkv_ref[0] = (dot(n1, wqkv_ref[...]) + bias_ref[...]).astype(bf16)
    keys_extra = key_lanes()
    for pair in range(HEADS // 2):
        at = 128 * pair
        q = qkv_ref[0, :, at : at + 128]
        key = jnp.concatenate([qkv_ref[0, :, D + at : D + at + 128], keys_extra], axis=1)
        v_t = qkv_ref[0, :, 2 * D + at : 2 * D + at + 128].T
        tables = dot(q, tab_ref[...])
        outs = []
        for head in range(2):
            extra = query_lanes(tables[:, 128 * head : 128 * head + 128])
            q_all = jnp.concatenate([q * (lane_mask(head) * 0.125), extra], axis=1)
            s_t = dot_nt(key, q_all)
            e = jnp.exp(s_t - jnp.max(s_t, axis=0, keepdims=True))
            p_t = (e * (1.0 / jnp.sum(e, axis=0, keepdims=True))).astype(bf16)
            pt_ref[0, 2 * pair + head] = p_t
            outs.append(dot(v_t[HD * head : HD * head + HD], p_t))
        o_ref[0, :, at : at + 128] = jnp.concatenate(outs, axis=0).T.astype(bf16)
    a = dot(o_ref[0], wproj_ref[...]) + vec[6:7]
    h = mask * (big + a)
    h_ref[0] = h
    normed_two, _ = norm_parts(h)
    n2_ref[0] = (mask * (normed_two * vec[1:2] + vec[3:4])).astype(bf16)


def forward_attention(info, x_slots, prev, nxt, w_qkv, w_proj, vec, bias, tab):
    windows = info.shape[0]
    one = lambda *tail: pl.BlockSpec((1,) + tail, lambda k, s: (k,) + (0,) * len(tail))
    whole = lambda a: pl.BlockSpec(a.shape, lambda k, s: (0,) * a.ndim)
    shape = lambda *tail, dtype=bf16: jax.ShapeDtypeStruct((windows,) + tail, dtype)
    return pl.pallas_call(
        fwd_kernel,
        grid_spec=pltpu.PrefetchScalarGridSpec(
            num_scalar_prefetch=1,
            grid=(windows,),
            in_specs=[
                pl.BlockSpec((1, TOKW, D), lambda k, s: (s[k, 0], 0, 0)),
                whole(prev), whole(nxt), whole(w_qkv), whole(w_proj), whole(vec), whole(bias), whole(tab),
            ],
            out_specs=[
                one(TP, D), one(TP, D), one(TP, 3 * D), one(HEADS, TP, TP), one(TP, D), one(TP, D), one(TP, D),
            ],
        ),
        out_shape=[
            shape(TP, D), shape(TP, D), shape(TP, 3 * D), shape(HEADS, TP, TP), shape(TP, D),
            shape(TP, D, dtype=f32), shape(TP, D),
        ],
        compiler_params=pltpu.CompilerParams(vmem_limit_bytes=VMEM_LIMIT),
        cost_estimate=pl.CostEstimate(flops=12 * 10**9, bytes_accessed=20 * 10**6, transcendentals=2 * 10**6),
        name="attention_forward",
    )(info, x_slots, prev, nxt, w_qkv, w_proj, vec, bias, tab)


def prepare(small):
    s = small.astype(f32)
    vec = s[: 8 * D].reshape(8, D)
    first_bias = s[8 * D : 8 * D + FF].reshape(1, FF)
    bias = jnp.concatenate([vec[4:5], jnp.zeros((1, D), f32), vec[5:6]], axis=1)
    tables = small[8 * D + FF :].reshape(2, RELN, HD)
    back_h, back_w, rel_w = tables[0, ::-1], tables[1, ::-1], tables[1]
    gap = jnp.zeros((64 - RELN, HD), bf16)
    one = jnp.concatenate([back_w, gap, back_h, gap], axis=0)
    none = jnp.zeros_like(one)
    fwd = jnp.block([[one.T, none.T], [none.T, one.T]])
    short = jnp.zeros((32 - RELN, HD), bf16)
    half = jnp.concatenate([back_h, short, rel_w, short], axis=0)
    nil = jnp.zeros_like(half)
    bwd = jnp.block([[nil, half], [half, nil]])
    return vec, first_bias, bias, fwd, bwd


def params(flops, moved, trans=0, **more):
    return dict(
        compiler_params=pltpu.CompilerParams(vmem_limit_bytes=VMEM_LIMIT),
        cost_estimate=pl.CostEstimate(flops=flops, bytes_accessed=moved, transcendentals=trans),
        **more,
    )


def whole(a):
    return pl.BlockSpec(a.shape, lambda k, *s: (0,) * a.ndim)


def sds(*dims, dtype=bf16):
    return jax.ShapeDtypeStruct(dims, dtype)


def masks(info, windows):
    return [inside(info[k, 2], info[k, 3]) for k in range(windows)]


def up_kernel(info, n2_ref, cot_ref, w1_ref, b1_ref, gl_ref, slope_ref, grad_ref, dz_ref, b2_ref, dz_t):
    windows = cot_ref.shape[0]

    @pl.when(pl.program_id(0) == 0)
    def _():
        total = jnp.zeros((1, D), f32)
        for k, mask in enumerate(masks(info, windows)):
            part = dot(spread(), cot_ref[k]) * mask
            dz_ref[TP * k : TP * k + TP] = part.astype(bf16)
            total += jnp.sum(part, axis=0, keepdims=True)
        b2_ref[...] = total
        dz_t[...] = dz_ref[...].T

    u = dot(n2_ref[...], w1_ref[...]) + b1_ref[...]
    half = 0.5 * (1.0 + lax.erf(u * root_half))
    gl = (u * half).astype(bf16)
    gl_ref[...] = gl
    slope_ref[...] = (half + u * jnp.exp(-0.5 * u * u) * inv_root_two_pi).astype(bf16)
    grad = dot(dz_t[...], gl).astype(bf16)
    for g in range(grad_ref.shape[0]):
        rows = grad_ref.shape[2]
        for w in range(grad_ref.shape[1]):
            cols = grad_ref.shape[3]
            grad_ref[g, w] = grad[rows * g : rows * g + rows, cols * w : cols * w + cols]


def feed_up(info, n2, cot, w_fc1, b1):
    rows = n2.shape[0]
    step = D
    steps = FF // step
    return pl.pallas_call(
        up_kernel,
        grid_spec=pltpu.PrefetchScalarGridSpec(
            num_scalar_prefetch=1,
            grid=(steps,),
            in_specs=[
                whole(n2), whole(cot),
                pl.BlockSpec((D, step), lambda k, s: (0, k)),
                pl.BlockSpec((1, step), lambda k, s: (0, k)),
            ],
            out_specs=[
                pl.BlockSpec((rows, step), lambda k, s: (0, k)),
                pl.BlockSpec((rows, step), lambda k, s: (0, k)),
                pl.BlockSpec((4, 2, 192, 384), lambda k, s: (0, k, 0, 0)),
                pl.BlockSpec((rows, D), lambda k, s: (0, 0)),
                pl.BlockSpec((1, D), lambda k, s: (0, 0)),
            ],
            scratch_shapes=[pltpu.VMEM((D, rows), bf16)],
        ),
        out_shape=[
            sds(rows, FF), sds(rows, FF), sds(4, 8, 192, 384), sds(rows, D), sds(1, D, dtype=f32),
        ],
        name="feed_up",
        **params(6 * 10**9, 24 * 10**6, 4 * 10**6),
    )(info, n2, cot, w_fc1, b1)


def down_kernel(
    info, dz_ref, slope_ref, n2_ref, h_ref, w1_ref, w2_ref, wproj_ref, vec_ref,
    grad_ref, b1_ref, dh_ref, da_ref, do_ref, sums_ref, n2_t, acc,
):
    step = pl.program_id(0)

    @pl.when(step == 0)
    def _():
        n2_t[...] = n2_ref[...].T
        acc[...] = jnp.zeros_like(acc)

    du = dot_nt(dz_ref[...], w2_ref[...]) * slope_ref[...].astype(f32)
    du_low = du.astype(bf16)
    b1_ref[...] = jnp.sum(du_low.astype(f32), axis=0, keepdims=True)
    grad_ref[0] = dot(n2_t[...], du_low).astype(bf16)
    acc[...] += dot_nt(du_low, w1_ref[...])

    @pl.when(step == pl.num_programs(0) - 1)
    def _():
        vec = vec_ref[...]
        windows = acc.shape[0] // TP
        gain = jnp.zeros((1, D), f32)
        shift = jnp.zeros((1, D), f32)
        bias = jnp.zeros((1, D), f32)
        for k, mask in enumerate(masks(info, windows)):
            at = slice(TP * k, TP * k + TP)
            dn = acc[at] * mask
            normed, scale_inv = norm_parts(h_ref[at])
            gain += jnp.sum(dn * normed, axis=0, keepdims=True)
            shift += jnp.sum(dn, axis=0, keepdims=True)
            dh = mask * (dz_ref[at].astype(f32) + norm_back(dn * vec[1:2], normed, scale_inv))
            dh_ref[at] = dh
            da = dh.astype(bf16)
            da_ref[at] = da
            bias += jnp.sum(da.astype(f32), axis=0, keepdims=True)
            do_ref[at] = dot_nt(da, wproj_ref[...]).astype(bf16)
        sums_ref[0:1] = gain
        sums_ref[1:2] = shift
        sums_ref[2:3] = bias
        sums_ref[3:8] = jnp.zeros((5, D), f32)


def feed_down(info, dz, slope, n2, h, w_fc1, w_fc2, w_proj, vec):
    rows = n2.shape[0]
    step = D
    steps = FF // step
    return pl.pallas_call(
        down_kernel,
        grid_spec=pltpu.PrefetchScalarGridSpec(
            num_scalar_prefetch=1,
            grid=(steps,),
            in_specs=[
                whole(dz),
                pl.BlockSpec((rows, step), lambda k, s: (0, k)),
                whole(n2), whole(h),
                pl.BlockSpec((D, step), lambda k, s: (0, k)),
                pl.BlockSpec((step, D), lambda k, s: (k, 0)),
                whole(w_proj), whole(vec),
            ],
            out_specs=[
                pl.BlockSpec((1, D, step), lambda k, s: (k, 0, 0)),
                pl.BlockSpec((1, step), lambda k, s: (0, k)),
                pl.BlockSpec((rows, D), lambda k, s: (0, 0)),
                pl.BlockSpec((rows, D), lambda k, s: (0, 0)),
                pl.BlockSpec((rows, D), lambda k, s: (0, 0)),
                pl.BlockSpec((8, D), lambda k, s: (0, 0)),
            ],
            scratch_shapes=[pltpu.VMEM((D, rows), bf16), pltpu.VMEM((rows, D), f32)],
        ),
        out_shape=[
            sds(4, D, D), sds(1, FF, dtype=f32), sds(rows, D, dtype=f32), sds(rows, D), sds(rows, D),
            sds(8, D, dtype=f32),
        ],
        name="feed_down",
        **params(9 * 10**9, 24 * 10**6),
    )(info, dz, slope, n2, h, w_fc1, w_fc2, w_proj, vec)


def out_kernel(info, gl_ref, w2_ref, h_ref, vec_ref, out_ref, acc):
    step = pl.program_id(0)

    @pl.when(step == 0)
    def _():
        acc[...] = h_ref[...]

    acc[...] += dot(gl_ref[...], w2_ref[...])

    @pl.when(step == pl.num_programs(0) - 1)
    def _():
        for k, mask in enumerate(masks(info, out_ref.shape[0])):
            at = slice(TP * k, TP * k + TP)
            y = (mask * (acc[at] + vec_ref[7:8])).astype(bf16)
            out_ref[k] = dot(gather_rows(), y).astype(bf16)


def feed_out(info, gl, w_fc2, h, vec):
    rows = gl.shape[0]
    windows = rows // TP
    step = D
    return pl.pallas_call(
        out_kernel,
        grid_spec=pltpu.PrefetchScalarGridSpec(
            num_scalar_prefetch=1,
            grid=(FF // step,),
            in_specs=[
                pl.BlockSpec((rows, step), lambda k, s: (0, k)),
                pl.BlockSpec((step, D), lambda k, s: (k, 0)),
                whole(h), whole(vec),
            ],
            out_specs=pl.BlockSpec((windows, TOKW, D), lambda k, s: (0, 0, 0)),
            scratch_shapes=[pltpu.VMEM((rows, D), f32)],
        ),
        out_shape=sds(windows, TOKW, D),
        name="feed_out",
        **params(3 * 10**9, 12 * 10**6),
    )(info, gl, w_fc2, h, vec)


def key_rows():
    lane, col = iota((64, TP), 0), iota((64, TP), 1)
    i, j = col >> 4, col & 15
    hit = ((lane < WS) & (lane == i)) | ((lane >= 32) & (lane < 32 + WS) & (lane - 32 == 13 - j))
    return hit.astype(f32).astype(bf16)


def grad_rolls(table, base):
    lane = iota((16, 128), 1)
    out = []
    for i in range(WS):
        tile = table[16 * i : 16 * i + 16]
        by_row = jnp.where((lane >= base) & (lane < base + WS), tile, 0.0)
        by_row = pltpu.roll(by_row, 13 - i, 1) if i < 13 else by_row
        by_col = jnp.where((lane >= base + 32) & (lane < base + 32 + WS), tile, 0.0)
        out.append(by_row + pltpu.roll(by_col, 0, 1, stride=1, stride_axis=0))
    return jnp.concatenate(out, axis=0)


def back_kernel(qkv_ref, pt_ref, do_ref, tab_ref, dqkv_ref, table_ref, sums_ref):
    @pl.when(pl.program_id(0) == 0)
    def _():
        table_ref[...] = jnp.zeros_like(table_ref)
        sums_ref[...] = jnp.zeros_like(sums_ref)

    rows_extra = key_rows()
    lane = iota((TP, 128), 1)
    for pair in range(HEADS // 2):
        at = 128 * pair
        q = qkv_ref[0, :, at : at + 128]
        key_t = (qkv_ref[0, :, D + at : D + at + 128] * jnp.asarray(0.125, bf16)).T
        v = qkv_ref[0, :, 2 * D + at : 2 * D + at + 128]
        do = do_ref[0, :, at : at + 128]
        ds_all, dq_all, z_all = [], [], []
        for head in range(2):
            p_t = pt_ref[0, 2 * pair + head].astype(f32)
            dp_t = dot_nt(v, do * lane_mask(head))
            mean = jnp.sum(p_t * dp_t, axis=0, keepdims=True) / jnp.sum(p_t, axis=0, keepdims=True)
            ds_t = (p_t * (dp_t - mean)).astype(bf16)
            ds_all.append(ds_t)
            if head == 0:
                left = jnp.concatenate([key_t[:HD], rows_extra], axis=0)
            else:
                left = jnp.concatenate([rows_extra, key_t[HD:]], axis=0)
            back = dot(left, ds_t).T
            dq_all.append(back)
            z_all.append(grad_rolls(back, 64 if head == 0 else 0))
        z = jnp.where(lane < HD, z_all[1], z_all[0]).astype(bf16)
        dq = jnp.where(lane < HD, dq_all[0], dq_all[1]) + dot(z, tab_ref[...])
        table_ref[...] += dot(z.T, q)
        two = lambda a: jnp.concatenate([a * lane_mask(0), a * lane_mask(1)], axis=0)
        dk = dot(jnp.concatenate(ds_all, axis=1), two(q)) * 0.125
        p_two = jnp.concatenate([pt_ref[0, 2 * pair], pt_ref[0, 2 * pair + 1]], axis=1)
        dv = dot(p_two, two(do))
        dqkv_ref[0, :, at : at + 128] = dq.astype(bf16)
        dqkv_ref[0, :, D + at : D + at + 128] = dk.astype(bf16)
        dqkv_ref[0, :, 2 * D + at : 2 * D + at + 128] = dv.astype(bf16)
    sums_ref[...] += jnp.sum(dqkv_ref[0].astype(f32), axis=0, keepdims=True)


def backward_attention(qkv, p_t, do, tab):
    windows = qkv.shape[0]
    one = lambda *tail: pl.BlockSpec((1,) + tail, lambda k: (k,) + (0,) * len(tail))
    return pl.pallas_call(
        back_kernel,
        grid=(windows,),
        in_specs=[one(TP, 3 * D), one(HEADS, TP, TP), one(TP, D), whole(tab)],
        out_specs=[
            one(TP, 3 * D),
            pl.BlockSpec((128, 128), lambda k: (0, 0)),
            pl.BlockSpec((1, 3 * D), lambda k: (0, 0)),
        ],
        out_shape=[sds(windows, TP, 3 * D), sds(128, 128, dtype=f32), sds(1, 3 * D, dtype=f32)],
        name="attention_backward",
        **params(8 * 10**9, 16 * 10**6),
    )(qkv, p_t, do, tab)


def last_kernel(
    info, n1_ref, dqkv_ref, o_ref, da_ref, wqkv_ref, xpad_ref, dh_ref, vec_ref,
    grad_ref, dx_ref, sums_ref, n1_t, o_t, acc,
):
    step = pl.program_id(0)

    @pl.when(step == 0)
    def _():
        n1_t[...] = n1_ref[...].T
        o_t[...] = o_ref[...].T
        acc[...] = jnp.zeros_like(acc)

    dqkv = dqkv_ref[...]
    part = dot(n1_t[...], dqkv)
    proj = dot(o_t[...], da_ref[...])
    lane = iota((D, 128), 1) < 64
    low = lambda a: a.astype(bf16)
    grad_ref[0, :, 0:512] = low(part[:, 0:512])
    moved = pltpu.roll(proj[:, 0:256], 64, 1)
    grad_ref[0, :, 512:640] = low(jnp.where(lane, part[:, 512:640], moved[:, 0:128]))
    grad_ref[0, :, 640:768] = low(moved[:, 128:256])
    rolled = pltpu.roll(part[:, 512:1152], 576, 1)
    grad_ref[1, :, 0:512] = low(rolled[:, 0:512])
    grad_ref[1, :, 512:640] = low(jnp.where(lane, rolled[:, 512:640], proj[:, 128:256]))
    grad_ref[1, :, 640:768] = low(proj[:, 256:384])
    acc[...] += dot_nt(dqkv, wqkv_ref[...])

    @pl.when(step == pl.num_programs(0) - 1)
    def _():
        vec = vec_ref[...]
        gain = jnp.zeros((1, D), f32)
        shift = jnp.zeros((1, D), f32)
        for k, mask in enumerate(masks(info, dx_ref.shape[0])):
            at = slice(TP * k, TP * k + TP)
            dn = acc[at] * mask
            normed, scale_inv = norm_parts(xpad_ref[at].astype(f32))
            gain += jnp.sum(dn * normed, axis=0, keepdims=True)
            shift += jnp.sum(dn, axis=0, keepdims=True)
            dx = dh_ref[at] + norm_back(dn * vec[0:1], normed, scale_inv)
            dx_ref[k] = dot(gather_rows(), dx.astype(bf16)).astype(bf16)
        sums_ref[0:1] = gain
        sums_ref[1:2] = shift
        sums_ref[2:8] = jnp.zeros((6, D), f32)


def backward_last(info, n1, dqkv, o, da, w_qkv, xpad, dh, vec):
    rows = n1.shape[0]
    windows = rows // TP
    wide = 3 * D // 2
    return pl.pallas_call(
        last_kernel,
        grid_spec=pltpu.PrefetchScalarGridSpec(
            num_scalar_prefetch=1,
            grid=(2,),
            in_specs=[
                whole(n1),
                pl.BlockSpec((rows, wide), lambda k, s: (0, k)),
                whole(o),
                pl.BlockSpec((rows, D // 2), lambda k, s: (0, k)),
                pl.BlockSpec((D, wide), lambda k, s: (0, k)),
                whole(xpad), whole(dh), whole(vec),
            ],
            out_specs=[
                pl.BlockSpec((2, D, D), lambda k, s: (k, 0, 0)),
                pl.BlockSpec((windows, TOKW, D), lambda k, s: (0, 0, 0)),
                pl.BlockSpec((8, D), lambda k, s: (0, 0)),
            ],
            scratch_shapes=[
                pltpu.VMEM((D, rows), bf16), pltpu.VMEM((D, rows), bf16), pltpu.VMEM((rows, D), f32),
            ],
        ),
        out_shape=[sds(4, D, D), sds(windows, TOKW, D), sds(8, D, dtype=f32)],
        name="backward_last",
        **params(6 * 10**9, 20 * 10**6),
    )(info, n1, dqkv, o, da, w_qkv, xpad, dh, vec)


def device_step(info, x_slots, prev, nxt, cot, w_qkv, w_proj, w_fc1, w_fc2, small):
    vec, b1, bias, tab_fwd, tab_bwd = prepare(small)
    xpad, n1, qkv, p_t, o, h, n2 = forward_attention(
        info, x_slots, prev, nxt, w_qkv, w_proj, vec, bias, tab_fwd
    )
    rows = xpad.shape[0] * TP
    flat = lambda a: a.reshape(rows, a.shape[2])
    gl, slope, grad_fc2, dz, sum_b2 = feed_up(info, flat(n2), cot, w_fc1, b1)
    grad_fc1, sum_b1, dh, da, do, sums_two = feed_down(
        info, dz, slope, flat(n2), flat(h), w_fc1, w_fc2, w_proj, vec
    )
    block_out = feed_out(info, gl, w_fc2, flat(h), vec)
    dqkv, table, sum_qkv = backward_attention(qkv, p_t, do.reshape(-1, TP, D), tab_bwd)
    grad_attn, dx, sums_one = backward_last(
        info, flat(n1), flat(dqkv), flat(o), da, w_qkv, flat(xpad), dh, vec
    )
    rel_h = (table[0:RELN, 64:] + table[64 : 64 + RELN, :64])[::-1]
    rel_w = table[32 : 32 + RELN, 64:] + table[96 : 96 + RELN, :64]
    small_grad = jnp.concatenate(
        [
            sums_one[0], sums_two[0], sums_one[1], sums_two[1], sum_qkv[0, :D], sum_qkv[0, 2 * D :],
            sums_two[2], sum_b2[0], sum_b1[0], rel_h.reshape(-1), rel_w.reshape(-1),
        ]
    )
    return block_out, dx, grad_fc2, grad_fc1, grad_attn, small_grad


def slots_kernel(info, dx_ref, prev_ref, next_ref, out_ref):
    source = info[pl.program_id(0), 1]
    zero = jnp.zeros_like(dx_ref[0])
    out_ref[0] = jnp.where(
        source == 0,
        dx_ref[0],
        jnp.where(source == 1, prev_ref[0], jnp.where(source == 2, next_ref[0], zero)),
    )


def to_slots(info, dx, prev, nxt):
    slots = info.shape[0]
    return pl.pallas_call(
        slots_kernel,
        grid_spec=pltpu.PrefetchScalarGridSpec(
            num_scalar_prefetch=1,
            grid=(slots,),
            in_specs=[pl.BlockSpec((1, TOKW, D), lambda k, s: (s[k, 0], 0, 0)), whole(prev), whole(nxt)],
            out_specs=pl.BlockSpec((1, TOKW, D), lambda k, s: (k, 0, 0)),
        ),
        out_shape=sds(slots, TOKW, D),
        name="to_slots",
        **params(10**6, 3 * 10**6),
    )(info, dx, prev, nxt)


AXES = ("win", "grp")


def bits_of(size):
    return [1 << k for k in range(size.bit_length() - 1)]


def flipped(axis, bit):
    wins, grps = lax.axis_size("win"), lax.axis_size("grp")
    out = []
    for d in range(wins * grps):
        w, g = divmod(d, grps)
        w, g = (w ^ bit, g) if axis == "win" else (w, g ^ bit)
        out.append((d, w * grps + g))
    return out


def windows_before(count):
    total, before = count, jnp.zeros_like(count)
    for axis in ("grp", "win"):
        for bit in bits_of(lax.axis_size(axis)):
            other = lax.ppermute(total, AXES, flipped(axis, bit))
            mine = (lax.axis_index(axis) & bit) != 0
            before = before + jnp.where(mine, other, 0)
            total = total + other
    return before


def neighbours(last, first):
    count = lax.axis_size("win") * lax.axis_size("grp")
    up = [(i, i + 1) for i in range(count - 1)]
    down = [(j, i) for i, j in up]
    return lax.ppermute(last, AXES, up), lax.ppermute(first, AXES, down)


def rising():
    return [(axis, bit) for axis in ("grp", "win") for bit in bits_of(lax.axis_size(axis))]


def reduce_scatter(grad, order):
    rows, columns = grad.shape[2:]
    parts = [
        (axis, bit) for axis in ("grp", "win") for bit in reversed(bits_of(lax.axis_size(axis)))
    ]
    kept = grad.reshape((2,) * len(parts) + (rows, columns))
    came = None
    for axis, bit in order:
        at = parts.index((axis, bit))
        mine = ((lax.axis_index(axis) & bit) != 0).astype(jnp.int32)

        def pick(half):
            piece = lax.dynamic_index_in_dim(kept, half, at, keepdims=False)
            if came is None:
                return piece
            other = lax.dynamic_index_in_dim(came, half, at, keepdims=False)
            return (piece.astype(f32) + other.astype(f32)).astype(bf16)

        send, kept = pick(1 - mine), pick(mine)
        came = lax.ppermute(send, AXES, flipped(axis, bit))
        parts.pop(at)
    return kept.astype(f32) + came.astype(f32)


def gather_win(block, order):
    have = block[None]
    for axis, bit in order:
        have = jnp.concatenate([have, lax.ppermute(have, AXES, flipped(axis, bit))], axis=0)
    place = lax.axis_index("win")
    out = []
    for target in range(have.shape[0]):
        apart = place ^ target
        at = sum(jnp.where((apart & bit) != 0, 1 << k, 0) for k, (_, bit) in enumerate(order))
        out.append(lax.dynamic_index_in_dim(have, at, 0, keepdims=False))
    return jnp.stack(out)


def adam_step(parameter, gradient, moment, square):
    first_fix = 1.0 - jnp.power(jnp.float32(0.5), jnp.float32(STEP))
    second_fix = 1.0 - jnp.power(jnp.float32(0.999), jnp.float32(STEP))
    moment_next = 0.5 * moment + 0.5 * gradient
    square_next = 0.999 * square + 0.001 * gradient * gradient
    fresh_weight = parameter - learn_rate * (moment_next / first_fix) / (
        jnp.sqrt(square_next / second_fix) + 1e-08
    )
    return (moment_next, square_next, fresh_weight.astype(bf16))


def per_device(
    x_slots, counts, cotangent, w_qkv, w_proj, w_fc1, w_fc2, small_params,
    moment_qkv, moment_proj, moment_fc1, moment_fc2, moment_small,
    square_qkv, square_proj, square_fc1, square_fc2, square_small,
):
    slots, per_even = x_slots.shape[0], cotangent.shape[0]
    win_at, grp_at = lax.axis_index("win"), lax.axis_index("grp")
    wins, grps = lax.axis_size("win"), lax.axis_size("grp")
    base = (win_at * grps + grp_at) * per_even
    count = counts[0]
    prev, nxt = neighbours(lax.dynamic_slice_in_dim(x_slots, count - 1, 1, 0), x_slots[:1])
    offset = windows_before(counts)[0]
    window = base + jnp.arange(per_even, dtype=jnp.int32)
    slot = window - offset
    spot = window % (GRID * GRID)
    info = jnp.stack(
        [
            jnp.clip(slot, 0, slots - 1),
            jnp.where(slot < 0, 1, jnp.where(slot >= count, 2, 0)),
            SIDE - WS * (spot // GRID),
            SIDE - WS * (spot % GRID),
        ],
        axis=1,
    ).astype(jnp.int32)
    block_out, dx, grad_fc2, grad_fc1, grad_attn, small_grad = device_step(
        info, x_slots, prev, nxt, cotangent, w_qkv, w_proj, w_fc1, w_fc2, small_params
    )
    dx_prev, dx_next = neighbours(dx[per_even - 1 :], dx[:1])
    place = offset + jnp.arange(slots, dtype=jnp.int32) - base
    live = jnp.arange(slots) < count
    back = jnp.where(place < 0, 1, jnp.where(place >= per_even, 2, 0))
    back = jnp.stack([jnp.clip(place, 0, per_even - 1), jnp.where(live, back, 3)], axis=1)
    input_grad = to_slots(back.astype(jnp.int32), dx, dx_prev, dx_next)

    blocks = lambda grad: grad.reshape(grps, wins, D // wins, D)
    fc2_blocks = grad_fc2
    if wins != grad_fc2.shape[1]:
        flat = grad_fc2.transpose(0, 2, 1, 3).reshape(grps, D // grps, wins, FF // wins)
        fc2_blocks = flat.transpose(0, 2, 1, 3)
    part_d = reduce_scatter(fc2_blocks, rising()).T
    part_c = reduce_scatter(blocks(grad_fc1), rising())
    part_ab = reduce_scatter(blocks(grad_attn), rising())
    part_a, part_b = part_ab[:, : 3 * D // grps], part_ab[:, 3 * D // grps :]
    grad_small = lax.psum(small_grad, AXES)

    def owned_part(weight, piece):
        return lax.dynamic_slice(
            weight, (win_at * piece.shape[0], grp_at * piece.shape[1]), piece.shape
        ).astype(f32)

    upd_qkv = adam_step(owned_part(w_qkv, part_a), part_a, moment_qkv, square_qkv)
    upd_proj = adam_step(owned_part(w_proj, part_b), part_b, moment_proj, square_proj)
    upd_fc1 = adam_step(owned_part(w_fc1, part_c), part_c, moment_fc1, square_fc1)
    upd_fc2 = adam_step(owned_part(w_fc2, part_d), part_d, moment_fc2, square_fc2)
    upd_small = adam_step(small_params.astype(f32), grad_small, moment_small, square_small)
    order = [one for one in reversed(rising()) if one[0] == "win"]
    new_fc2 = gather_win(upd_fc2[2].T, order).transpose(0, 2, 1).reshape(FF, D // grps)
    new_fc1 = gather_win(upd_fc1[2], order).reshape(D, FF // grps)
    both = gather_win(jnp.concatenate([upd_qkv[2], upd_proj[2]], axis=1), order).reshape(D, D)
    new_qkv, new_proj = both[:, : 3 * D // grps], both[:, 3 * D // grps :]
    return (
        block_out, input_grad, part_a, part_b, part_c, part_d, grad_small,
        upd_qkv[0], upd_proj[0], upd_fc1[0], upd_fc2[0], upd_small[0],
        upd_qkv[1], upd_proj[1], upd_fc1[1], upd_fc2[1], upd_small[1],
        new_qkv, new_proj, new_fc1, new_fc2, upd_small[2],
    )


def solution(mesh):
    data, shard, same, part = P(AXES, None, None), P("win", "grp"), P(), P(None, "grp")
    in_specs = (data, P(AXES), data) + (same,) * 5 + ((shard,) * 4 + (same,)) * 2
    out_specs = (data,) * 2 + ((shard,) * 4 + (same,)) * 3 + (part,) * 4 + (same,)
    return jax.shard_map(
        per_device, mesh=mesh, in_specs=in_specs, out_specs=out_specs, check_vma=False
    )
```

time: 1120 us -> 420 us (0.38)
  local copies, waits for them, and re-layouts: 317 us -> 35.7 us
  waiting for transfers between devices: 288 us -> 88.4 us
  matrix products: 198 us -> 0 us
  Pallas kernels: 0 us -> 107 us
  other arithmetic: 139 us -> 32.7 us
  blocking collectives: 149 us -> 95.6 us
  starting transfers between devices: 5.95 us -> 44.6 us
    reduce_scatter x5 -> x0, waiting for transfers between devices: 233 us -> none  [the longest x1 127 us: per_device(): lax.psum_scatter(grad_qkv, 'win', scatter_dimension=0, tiled=True)]
    dot_general x28 -> x0, matrix products: 198 us -> none  [the longest x4 34.7 us: contract_cols(): lax.dot_general(left_part, right_part, (((1,), (1,)), ((), ())), preferre...]
    reshape x21 -> x4, local copies, waits for them, and re-layouts: 139 us -> 3.28 us  [the longest x1 1.21 us: per_device(): gather_win(upd_fc2[2].T, order).transpose(0, 2, 1).reshape(FF, D // grps)]
    pallas_call x0 -> x7, Pallas kernels: none -> 107 us  [the longest x1 24.2 us: forward_attention(): pl.pallas_call(fwd_kernel, grid_spec=pltpu.PrefetchScalarGridSpec(num_sca...]
    ppermute x2 -> x33, waiting for transfers between devices: 0.01 us -> 88.4 us  [the longest x9 47 us: gather_win(): lax.ppermute(have, AXES, flipped(axis, bit))]
    all_gather x2 -> x0, blocking collectives: 66.8 us -> none  [the longest x1 35.4 us: per_device(): lax.all_gather(upd_qkv[2], 'win', axis=0, tiled=True)]
    reduce_sum x11 -> x0, other arithmetic: 63.8 us -> none  [the longest x1 36.5 us: attend_backward(): along_rows = jnp.sum(split_grad, axis=5)]
    add x10 -> x0, local copies, waits for them, and re-layouts: 59.5 us -> none  [the longest x1 55.4 us: attention_scores(): along_rows[:, :, :, :, :, None] + along_cols[:, :, :, :, None, :]]
  transfers between devices with their start and end apart: 12 -> 33, of which waited for: 5 -> 12; matrix products, arithmetic and copies ran while one was open for 34% -> 15% of each run, Pallas kernels for 0% -> 3%
where the time goes in v1:
time: 420 us; the launch traced here: 412 us
  Pallas kernels  107 us (25%)
  blocking collectives  95.6 us (23%)
  waiting for transfers between devices  88.4 us (21%)
  starting transfers between devices  44.6 us (11%)
  local copies, waits for them, and re-layouts  35.7 us (9%)
  other arithmetic  32.7 us (8%)
  between operations  8.17 us (2%)
    psum x1, blocking collectives, per_device(): grad_small = lax.psum(small_grad, AXES)  95.6 us
    ppermute x9, waiting for transfers between devices, gather_win(): lax.ppermute(have, AXES, flipped(axis, bit))  47 us
    ppermute x15, waiting for transfers between devices, reduce_scatter(): came = lax.ppermute(send, AXES, flipped(axis, bit))  41.4 us
    pallas_call x1, Pallas kernels, forward_attention(): pl.pallas_call(fwd_kernel, grid_spec=pltpu.PrefetchScalarGridSpec(num_sca...  24.2 us
    pallas_call x1, Pallas kernels, feed_down(): pl.pallas_call(down_kernel, grid_spec=pltpu.PrefetchScalarGridSpec(num_sc...  21.2 us
    ppermute x5, starting transfers between devices, windows_before(): other = lax.ppermute(total, AXES, flipped(axis, bit))  18.6 us
    pallas_call x1, Pallas kernels, backward_attention(): pl.pallas_call(back_kernel, grid=(windows,), in_specs=[one(TP, 3 * D), on...  17.1 us
    pallas_call x1, Pallas kernels, backward_last(): pl.pallas_call(last_kernel, grid_spec=pltpu.PrefetchScalarGridSpec(num_sc...  16.7 us
  transfers between devices with their start and end apart: 33, of which 12 were waited for; matrix products, arithmetic and copies ran while one was open for 15% of the time, Pallas kernels for 3%

profile of v1, /device:TPU:0, one launch (start us, length us, event | category | flops | bytes accessed | tf_op | source)
XLA Modules:
  0.0 411.7 jit_solution(7888243341740324513)
XLA Ops:
  3.0 2.0 collective-permute-start.5
  10.9 6.2 %collective-permute-start.1 = (s32[1]{0:T(128)}, s32[1]{0:T(128)}, u32[]{:S(2)}, u32[]{:S(2)}) collective-permute-start(s32[1]{0:T(128)} %add.565), channel_id=1, source_target_pairs={{0,2},{1,3},{2,0},{3,1},{4,6},{5,7},{6,4},{7,5},{8,10},{9,11},{10,... | collective-permute-start | bytes 20 | tf_op jit(solution)/shard_map/ppermute | solution.py:620
  18.4 3.9 collective-permute-start.2
  23.6 3.9 collective-permute-start.3
  28.8 4.1 collective-permute-start.4
  36.2 24.2 %attention_forward.1 = (bf16[3,224,768]{2,1,0:T(8,128)(2,1)}, bf16[3,224,768]{2,1,0:T(8,128)(2,1)}, bf16[3,224,2304]{2,1,0:T(8,128)(2,1)}, bf16[3,12,224,224]{3,...) custom-call(s32[3,4]{1,0:T(4,128)} %pad_add_fusion.info, ...), custom_call_target="tpu_custom_call" | custom-call | flops 12000000000 | bytes 20000000 | tf_op jit(solution)/shard_map/attention_forward/pallas_call | solution.py:155
  60.4 13.5 %feed_up.1 = (bf16[672,3072]{1,0:T(8,128)(2,1)}, bf16[672,3072]{1,0:T(8,128)(2,1)}, bf16[4,8,192,384]{3,2,1,0:T(8,128)(2,1)}, bf16[672,768]{1,0:T(8,128)(2,1)}, f32[1,768]{1,0:T(1,128)}) custom-call(s32[3,4]{1,0:T(4,128)} %pad_add_fusion.info, bf16[672,768]{1,0:T(8,128)(2,1)} %bitcast.205, bf16[3,196,768]{2,1,0:T(8,128)(2,1)} %cot_ref.1, ...), custom_call_target="tpu_custom_call" | custom-call | flops 6000000000 | bytes 24000000 | tf_op jit(solution)/shard_map/feed_up/pallas_call | solution.py:246
  74.0 21.2 %feed_down.1 = (bf16[4,768,768]{2,1,0:T(8,128)(2,1)}, f32[1,3072]{1,0:T(1,128)}, f32[672,768]{1,0:T(8,128)}, bf16[672,768]{1,0:T(8,128)(2,1)}, bf16[672,768]{1,0:T(8,128)(2,1)}, /*index=5*/f32[8,768]{1,0:T(8,128)}) custom-call(s32[3,4]{1,0:T(4,128)} %pad_add_fusion.info, bf16[672,768]{1,0:T(8,128)(2,1)} %get-tuple-element.52.dz_ref, ...), custom_call_target="tpu_custom_call" | custom-call | flops 8999999488 | bytes 24000000 | tf_op jit(solution)/shard_map/feed_down/pallas_call | solution.py:319
  95.2 17.1 %attention_backward.1 = (bf16[3,224,2304]{2,1,0:T(8,128)(2,1)}, f32[128,128]{1,0:T(8,128)}, f32[1,2304]{1,0:T(1,128)}) custom-call(bf16[3,224,2304]{2,1,0:T(8,128)(2,1)} %get-tuple-element.50.qkv_ref, bf16[3,12,224,224]{3,2,1,0:T(8,128)(2,1)} %get-tuple-element.51.pt_ref, bf16[3,224,768]{2,1,0:T(8,128)(2,1)} %bitcast.207, bf16[128,128]{1,0:T(8,128)(2,1)} %fusion.43.tab_ref), custom_call_target="tpu_custom_call" | custom-call | flops 8000000000 | bytes 16000000 | tf_op jit(solution)/shard_map/attention_backward/pallas_call | solution.py:454
  112.3 16.7 %backward_last.1 = (bf16[4,768,768]{2,1,0:T(8,128)(2,1)}, bf16[3,196,768]{2,1,0:T(8,128)(2,1)}, f32[8,768]{1,0:T(8,128)}) custom-call(s32[3,4]{1,0:T(4,128)} %pad_add_fusion.info, bf16[672,768]{1,0:T(8,128)(2,1)} %bitcast.203, bf16[672,2304]{1,0:T(8,128)(2,1)} %bitcast.201, bf16[672,768]{1,0:T(8,128)(2,1)} %bitcast.204, ...), custom_call_target="tpu_custom_call" | custom-call | flops 6000000000 | bytes 20000000 | tf_op jit(solution)/shard_map/backward_last/pallas_call | solution.py:518
  129.0 3.5 copy_bitcast_fusion.2
  132.5 1.6 copy_bitcast_fusion.1
  134.6 1.7 copy_bitcast_fusion
  138.2 2.0 constant_dynamic-slice_fusion.8
  140.2 1.8 constant_dynamic-slice_fusion.5
  142.4 3.3 fusion.5
  146.0 3.3 fusion.3
  149.4 1.7 collective-permute-start.15
  151.1 3.3 fusion.1
  155.4 2.0 fusion.64
  157.4 2.3 collective-permute-start.7
  167.3 1.5 slice_reduce_fusion
  168.7 1.5 concatenate.81
  170.2 95.6 %psum.7 = f32[12672]{0:T(1024)} all-reduce(f32[12672]{0:T(1024)} %concatenate.81), channel_id=1, replica_groups=mesh['win'=8,'grp'=4] {'win','grp'}, use_global_device_ids=true, to_apply=%region_0.1 | all-reduce | flops 12672 | bytes 101376 | tf_op jit(solution)/shard_map/psum | solution.py:729
  265.8 1.5 add_convert_fusion.5
  267.4 2.3 collective-permute-start.11
  269.7 1.5 add_convert_fusion.3
  271.4 1.5 add_convert_fusion.1
  273.1 2.1 collective-permute-start.21
  275.8 8.2 %collective-permute-done.11 = bf16[2,2,96,768]{3,2,1,0:T(8,128)(2,1)S(1)} collective-permute-done((bf16[2,2,96,768]{3,2,1,0:T(8,128)(2,1)S(1)}, bf16[2,2,96,768]{3,2,1,0:T(8,128)(2,1)S(1)}, u32[]{:S(2)}, u32[]{:S(2)}) %collective-permute-start.11) | collective-permute-done | bytes 589856 | tf_op jit(solution)/shard_map/ppermute | solution.py:657
  284.5 12.1 %collective-permute-done.16 = bf16[2,2,96,768]{3,2,1,0:T(8,128)(2,1)S(1)} collective-permute-done((bf16[2,2,96,768]{3,2,1,0:T(8,128)(2,1)S(1)}, bf16[2,2,96,768]{3,2,1,0:T(8,128)(2,1)S(1)}, u32[]{:S(2)}, u32[]{:S(2)}) %collective-permute-start.16) | collective-permute-done | bytes 589856 | tf_op jit(solution)/shard_map/ppermute | solution.py:657
  297.1 10.2 %collective-permute-done.21 = bf16[2,2,192,384]{3,2,1,0:T(8,128)(2,1)S(1)} collective-permute-done((bf16[2,2,192,384]{3,2,1,0:T(8,128)(2,1)S(1)}, bf16[2,2,192,384]{3,2,1,0:T(8,128)(2,1)S(1)}, u32[]{:S(2)}, u32[]{:S(2)}) %collective-permute-start.21) | collective-permute-done | bytes 589856 | tf_op jit(solution)/shard_map/ppermute | solution.py:657
  308.0 9.2 %feed_out.1 = bf16[3,196,768]{2,1,0:T(8,128)(2,1)} custom-call(s32[3,4]{1,0:T(4,128)} %pad_add_fusion.info, bf16[672,3072]{1,0:T(8,128)(2,1)} %get-tuple-element.47.gl_ref, bf16[3072,768]{1,0:T(8,128)(2,1)} %w2_ref.3, f32[672,768]{1,0:T(8,128)} %bitcast.190, f32[8,768]{1,0:T(8,128)} %reshape.392.vec_ref), custom_call_target="tpu_custom_call" | custom-call | flops 3000000000 | bytes 12000000 | tf_op jit(solution)/shard_map/feed_out/pallas_call | solution.py:372
  317.2 4.7 %to_slots.1 = bf16[5,196,768]{2,1,0:T(8,128)(2,1)} custom-call(s32[5,2]{1,0:T(8,128)} %copy.82.info, bf16[3,196,768]{2,1,0:T(8,128)(2,1)} %get-tuple-element.60.dx_ref, bf16[1,196,768]{2,1,0:T(8,128)(2,1)} %collective-permute-done.7.prev_ref, bf16[1,196,768]{2,1,0:T(8,128)(2,1)} %collective-permute-done.8.next_ref), custom_call_target="tpu_custom_call" | custom-call | flops 1000000 | bytes 3000000 | tf_op jit(solution)/shard_map/to_slots/pallas_call | solution.py:585
  323.2 1.8 collective-permute-start.18
  326.3 10.9 %collective-permute-done.13 = bf16[96,768]{1,0:T(8,128)(2,1)S(1)} collective-permute-done((bf16[96,768]{1,0:T(8,128)(2,1)S(1)}, bf16[96,768]{1,0:T(8,128)(2,1)S(1)}, u32[]{:S(2)}, u32[]{:S(2)}) %collective-permute-start.13) | collective-permute-done | bytes 147488 | tf_op jit(solution)/shard_map/ppermute | solution.py:657
  337.3 1.9 subtract_convert_fusion.2
  339.2 1.7 subtract_convert_fusion.3
  341.1 2.0 fusion.35
  343.1 2.8 collective-permute-start.27
  348.6 6.7 %collective-permute-done.24 = bf16[1,96,768]{2,1,0:T(8,128)(2,1)S(1)} collective-permute-done((bf16[1,96,768]{2,1,0:T(8,128)(2,1)S(1)}, bf16[1,96,768]{2,1,0:T(8,128)(2,1)S(1)}, u32[]{:S(2)}, u32[]{:S(2)}) %collective-permute-start.24) | collective-permute-done | bytes 147488 | tf_op jit(solution)/shard_map/ppermute | solution.py:665
  355.4 3.1 collective-permute-done.27
  359.3 8.5 %collective-permute-done.25 = bf16[2,96,768]{2,1,0:T(8,128)(2,1)S(1)} collective-permute-done((bf16[2,96,768]{2,1,0:T(8,128)(2,1)S(1)}, bf16[2,96,768]{2,1,0:T(8,128)(2,1)S(1)}, u32[]{:S(2)}, u32[]{:S(2)}) %collective-permute-start.25) | collective-permute-done | bytes 294944 | tf_op jit(solution)/shard_map/ppermute | solution.py:665
  369.1 5.1 %collective-permute-done.28 = bf16[2,96,768]{2,1,0:T(8,128)(2,1)S(1)} collective-permute-done((bf16[2,96,768]{2,1,0:T(8,128)(2,1)S(1)}, bf16[2,96,768]{2,1,0:T(8,128)(2,1)S(1)}, u32[]{:S(2)}, u32[]{:S(2)}) %collective-permute-start.28) | collective-permute-done | bytes 294944 | tf_op jit(solution)/shard_map/ppermute | solution.py:665
  375.9 4.5 %collective-permute-done.31 = bf16[2,192,384]{2,1,0:T(8,128)(2,1)S(1)} collective-permute-done((bf16[2,192,384]{2,1,0:T(8,128)(2,1)S(1)}, bf16[2,192,384]{2,1,0:T(8,128)(2,1)S(1)}, u32[]{:S(2)}, u32[]{:S(2)}) %collective-permute-start.31) | collective-permute-done | bytes 294944 | tf_op jit(solution)/shard_map/ppermute | solution.py:665
  382.3 1.9 collective-permute-done.26
  384.3 12.5 %collective-permute-done.29 = bf16[4,96,768]{2,1,0:T(8,128)(2,1)S(1)} collective-permute-done((bf16[4,96,768]{2,1,0:T(8,128)(2,1)S(1)}, bf16[4,96,768]{2,1,0:T(8,128)(2,1)S(1)}, u32[]{:S(2)}, u32[]{:S(2)}) %collective-permute-start.29) | collective-permute-done | bytes 589856 | tf_op jit(solution)/shard_map/ppermute | solution.py:665
  403.9 4.7 %collective-permute-done.32 = bf16[4,192,384]{2,1,0:T(8,128)(2,1)} collective-permute-done((bf16[4,192,384]{2,1,0:T(8,128)(2,1)}, bf16[4,192,384]{2,1,0:T(8,128)(2,1)}, u32[]{:S(2)}, u32[]{:S(2)}) %collective-permute-start.32) | collective-permute-done | bytes 589856 | tf_op jit(solution)/shard_map/ppermute | solution.py:665
  (194 shorter events, 44.2 us)
Async XLA Ops:
  0.7 5.6 %copy-start.13 = (bf16[12672]{0:T(1024)(128)(2,1)S(1)}, bf16[12672]{0:T(1024)(128)(2,1)}, u32[]{:S(2)}) copy-start(bf16[12672]{0:T(1024)(128)(2,1)} %param.25) | copy-start | bytes 76036
  0.7 9.6 %collective-permute-start = (s32[1]{0:T(128)}, s32[1]{0:T(128)}, u32[]{:S(2)}, u32[]{:S(2)}) collective-permute-start(s32[1]{0:T(128)} %param.19), channel_id=1, source_target_pairs={{0,1},{1,0},{2,3},{3,2},{4,5},{5,4},{6,7},{7,6},{8,9},{9,8},{10,11... | collective-permute-start | bytes 20 | tf_op jit(solution)/shard_map/ppermute | solution.py:620
  3.0 31.8 %collective-permute-start.5 = (bf16[1,196,768]{2,1,0:T(8,128)(2,1)S(1)}, bf16[1,196,768]{2,1,0:T(8,128)(2,1)S(1)}, u32[]{:S(2)}, u32[]{:S(2)}) collective-permute-start(bf16[1,196,768]{2,1,0:T(8,128)(2,1)S(1)} %get-tuple-element.154), channel_id=1, source_target_pairs={{0,1},{1,2},{2,3},{3,4},{4,5},{5,6},{6,7},{7,8},{8,9},{9,10},{10,1... | collective-permute-start | bytes 903176 | tf_op jit(solution)/shard_map/ppermute | solution.py:631
  4.9 29.9 %collective-permute-start.6 = (bf16[1,196,768]{2,1,0:T(8,128)(2,1)S(1)}, bf16[1,196,768]{2,1,0:T(8,128)(2,1)S(1)}, u32[]{:S(2)}, u32[]{:S(2)}) collective-permute-start(bf16[1,196,768]{2,1,0:T(8,128)(2,1)S(1)} %get-tuple-element.153), channel_id=1, source_target_pairs={{1,0},{2,1},{3,2},{4,3},{5,4},{6,5},{7,6},{8,7},{9,8},{10,9},{11,1... | collective-permute-start | bytes 903176 | tf_op jit(solution)/shard_map/ppermute | solution.py:631
  10.9 6.8 %collective-permute-start.1 = (s32[1]{0:T(128)}, s32[1]{0:T(128)}, u32[]{:S(2)}, u32[]{:S(2)}) collective-permute-start(s32[1]{0:T(128)} %add.565), channel_id=1, source_target_pairs={{0,2},{1,3},{2,0},{3,1},{4,6},{5,7},{6,4},{7,5},{8,10},{9,11},{10,... | collective-permute-start | bytes 20 | tf_op jit(solution)/shard_map/ppermute | solution.py:620
  18.4 4.6 %collective-permute-start.2 = (s32[1]{0:T(128)}, s32[1]{0:T(128)}, u32[]{:S(2)}, u32[]{:S(2)}) collective-permute-start(s32[1]{0:T(128)} %add.567), channel_id=1, source_target_pairs={{0,4},{1,5},{2,6},{3,7},{4,0},{5,1},{6,2},{7,3},{8,12},{9,13},{10,... | collective-permute-start | bytes 20 | tf_op jit(solution)/shard_map/ppermute | solution.py:620
  23.6 4.5 %collective-permute-start.3 = (s32[1]{0:T(128)}, s32[1]{0:T(128)}, u32[]{:S(2)}, u32[]{:S(2)}) collective-permute-start(s32[1]{0:T(128)} %add.569), channel_id=1, source_target_pairs={{0,8},{1,9},{2,10},{3,11},{4,12},{5,13},{6,14},{7,15},{8,0},{9,1},... | collective-permute-start | bytes 20 | tf_op jit(solution)/shard_map/ppermute | solution.py:620
  28.8 4.7 %collective-permute-start.4 = (s32[1]{0:T(128)}, s32[1]{0:T(128)}, u32[]{:S(2)}, u32[]{:S(2)}) collective-permute-start(s32[1]{0:T(128)} %add.571), channel_id=1, source_target_pairs={{0,16},{1,17},{2,18},{3,19},{4,20},{5,21},{6,22},{7,23},{8,24},{9,... | collective-permute-start | bytes 20 | tf_op jit(solution)/shard_map/ppermute | solution.py:620
  95.2 39.5 %slice-start = ((s8[4718592]{0:T(1024)(128)(4,1)}), s8[4194304]{0:T(1024)(128)(4,1)S(1)}, s32[]{:S(2)}) async-start(s8[4718592]{0:T(1024)(128)(4,1)} %bitcast.179), calls=%async_computation | async-start | bytes 8388608
  112.3 22.4 %slice-start.1 = ((s8[4718592]{0:T(1024)(128)(4,1)}), s8[524288]{0:T(1024)(128)(4,1)S(1)}, s32[]{:S(2)}) async-start(s8[4718592]{0:T(1024)(128)(4,1)} %bitcast.179), calls=%async_computation.1 | async-start | bytes 1048576
  132.5 9.9 %collective-permute-start.9 = (bf16[2,2,2,2,96,768]{5,4,1,3,2,0:T(8,128)(2,1)}, bf16[2,2,2,2,96,768]{5,4,1,3,2,0:T(8,128)(2,1)}, u32[]{:S(2)}, u32[]{:S(2)}) collective-permute-start(bf16[2,2,2,2,96,768]{5,4,1,3,2,0:T(8,128)(2,1)} %copy_bitcast_fusion.2), channel_id=1, source_target_pairs={{0,1},{1,0},{2,3},{3,2},{4,5},{5,4},{6,7},{7,6},{8,9},{9,8},{10,11... | collective-permute-start | bytes 7077896 | tf_op jit(solution)/shard_map/ppermute | solution.py:657
  134.1 11.9 %collective-permute-start.14 = (bf16[2,2,2,2,96,768]{5,4,1,3,2,0:T(8,128)(2,1)}, bf16[2,2,2,2,96,768]{5,4,1,3,2,0:T(8,128)(2,1)}, u32[]{:S(2)}, u32[]{:S(2)}) collective-permute-start(bf16[2,2,2,2,96,768]{5,4,1,3,2,0:T(8,128)(2,1)} %copy_bitcast_fusion.1), channel_id=1, source_target_pairs={{0,1},{1,0},{2,3},{3,2},{4,5},{5,4},{6,7},{7,6},{8,9},{9,8},{10,11... | collective-permute-start | bytes 7077896 | tf_op jit(solution)/shard_map/ppermute | solution.py:657
  134.6 7.5 %slice-start.2 = ((s8[4718592]{0:T(1024)(128)(4,1)}), s8[524288]{0:T(1024)(128)(4,1)S(1)}, s32[]{:S(2)}) async-start(s8[4718592]{0:T(1024)(128)(4,1)} %bitcast.182), calls=%async_computation.2 | async-start | bytes 1048576
  136.3 14.8 %collective-permute-start.19 = (bf16[2,2,2,2,192,384]{5,4,1,3,2,0:T(8,128)(2,1)}, bf16[2,2,2,2,192,384]{5,4,1,3,2,0:T(8,128)(2,1)}, u32[]{:S(2)}, u32[]{:S(2)}) collective-permute-start(bf16[2,2,2,2,192,384]{5,4,1,3,2,0:T(8,128)(2,1)} %copy_bitcast_fusion), channel_id=1, source_target_pairs={{0,1},{1,0},{2,3},{3,2},{4,5},{5,4},{6,7},{7,6},{8,9},{9,8},{10,11... | collective-permute-start | bytes 7077896 | tf_op jit(solution)/shard_map/ppermute | solution.py:657
  145.7 120.1 %collective-permute-start.10 = (bf16[2,2,2,96,768]{4,3,0,2,1:T(8,128)(2,1)}, bf16[2,2,2,96,768]{4,3,0,2,1:T(8,128)(2,1)}, u32[]{:S(2)}, u32[]{:S(2)}) collective-permute-start(bf16[2,2,2,96,768]{4,3,0,2,1:T(8,128)(2,1)} %get-tuple-element.152), channel_id=1, source_target_pairs={{0,2},{1,3},{2,0},{3,1},{4,6},{5,7},{6,4},{7,5},{8,10},{9,11},{10,... | collective-permute-start | bytes 3538952 | tf_op jit(solution)/shard_map/ppermute | solution.py:657
  149.4 120.3 %collective-permute-start.15 = (bf16[2,2,2,96,768]{4,3,0,2,1:T(8,128)(2,1)}, bf16[2,2,2,96,768]{4,3,0,2,1:T(8,128)(2,1)}, u32[]{:S(2)}, u32[]{:S(2)}) collective-permute-start(bf16[2,2,2,96,768]{4,3,0,2,1:T(8,128)(2,1)} %get-tuple-element.148), channel_id=1, source_target_pairs={{0,2},{1,3},{2,0},{3,1},{4,6},{5,7},{6,4},{7,5},{8,10},{9,11},{10,... | collective-permute-start | bytes 3538952 | tf_op jit(solution)/shard_map/ppermute | solution.py:657
  154.4 117.0 %collective-permute-start.20 = (bf16[2,2,2,192,384]{4,3,0,2,1:T(8,128)(2,1)}, bf16[2,2,2,192,384]{4,3,0,2,1:T(8,128)(2,1)}, u32[]{:S(2)}, u32[]{:S(2)}) collective-permute-start(bf16[2,2,2,192,384]{4,3,0,2,1:T(8,128)(2,1)} %get-tuple-element.144), channel_id=1, source_target_pairs={{0,2},{1,3},{2,0},{3,1},{4,6},{5,7},{6,4},{7,5},{8,10},{9,11},{10,... | collective-permute-start | bytes 3538952 | tf_op jit(solution)/shard_map/ppermute | solution.py:657
  155.4 5.5 %copy-start.17 = (f32[128,128]{1,0:T(8,128)S(1)}, f32[128,128]{1,0:T(8,128)}, u32[]{:S(2)}) copy-start(f32[128,128]{1,0:T(8,128)} %get-tuple-element.69) | copy-start | bytes 196612
  157.4 159.8 %collective-permute-start.7 = (bf16[1,196,768]{2,1,0:T(8,128)(2,1)}, bf16[1,196,768]{2,1,0:T(8,128)(2,1)}, u32[]{:S(2)}, u32[]{:S(2)}) collective-permute-start(bf16[1,196,768]{2,1,0:T(8,128)(2,1)} %get-tuple-element.162), channel_id=1, source_target_pairs={{0,1},{1,2},{2,3},{3,4},{4,5},{5,6},{6,7},{7,8},{8,9},{9,10},{10,1... | collective-permute-start | bytes 903176 | tf_op jit(solution)/shard_map/ppermute | solution.py:631
  159.6 157.5 %collective-permute-start.8 = (bf16[1,196,768]{2,1,0:T(8,128)(2,1)}, bf16[1,196,768]{2,1,0:T(8,128)(2,1)}, u32[]{:S(2)}, u32[]{:S(2)}) collective-permute-start(bf16[1,196,768]{2,1,0:T(8,128)(2,1)} %get-tuple-element.161), channel_id=1, source_target_pairs={{1,0},{2,1},{3,2},{4,3},{5,4},{6,5},{7,6},{8,7},{9,8},{10,9},{11,1... | collective-permute-start | bytes 903176 | tf_op jit(solution)/shard_map/ppermute | solution.py:631
  267.4 16.6 %collective-permute-start.11 = (bf16[2,2,96,768]{3,2,1,0:T(8,128)(2,1)S(1)}, bf16[2,2,96,768]{3,2,1,0:T(8,128)(2,1)S(1)}, u32[]{:S(2)}, u32[]{:S(2)}) collective-permute-start(bf16[2,2,96,768]{3,2,1,0:T(8,128)(2,1)S(1)} %copy.86), channel_id=1, source_target_pairs={{0,4},{1,5},{2,6},{3,7},{4,0},{5,1},{6,2},{7,3},{8,12},{9,13},{10,... | collective-permute-start | bytes 1769480 | tf_op jit(solution)/shard_map/ppermute | solution.py:657
  271.3 25.3 %collective-permute-start.16 = (bf16[2,2,96,768]{3,2,1,0:T(8,128)(2,1)S(1)}, bf16[2,2,96,768]{3,2,1,0:T(8,128)(2,1)S(1)}, u32[]{:S(2)}, u32[]{:S(2)}) collective-permute-start(bf16[2,2,96,768]{3,2,1,0:T(8,128)(2,1)S(1)} %copy.91), channel_id=1, source_target_pairs={{0,4},{1,5},{2,6},{3,7},{4,0},{5,1},{6,2},{7,3},{8,12},{9,13},{10,... | collective-permute-start | bytes 1769480 | tf_op jit(solution)/shard_map/ppermute | solution.py:657
  273.1 34.3 %collective-permute-start.21 = (bf16[2,2,192,384]{3,2,1,0:T(8,128)(2,1)S(1)}, bf16[2,2,192,384]{3,2,1,0:T(8,128)(2,1)S(1)}, u32[]{:S(2)}, u32[]{:S(2)}) collective-permute-start(bf16[2,2,192,384]{3,2,1,0:T(8,128)(2,1)S(1)} %copy.96), channel_id=1, source_target_pairs={{0,4},{1,5},{2,6},{3,7},{4,0},{5,1},{6,2},{7,3},{8,12},{9,13},{10,... | collective-permute-start | bytes 1769480 | tf_op jit(solution)/shard_map/ppermute | solution.py:657
  284.1 37.8 %collective-permute-start.12 = (bf16[2,96,768]{2,1,0:T(8,128)(2,1)S(1)}, bf16[2,96,768]{2,1,0:T(8,128)(2,1)S(1)}, u32[]{:S(2)}, u32[]{:S(2)}) collective-permute-start(bf16[2,96,768]{2,1,0:T(8,128)(2,1)S(1)} %get-tuple-element.160), channel_id=1, source_target_pairs={{0,8},{1,9},{2,10},{3,11},{4,12},{5,13},{6,14},{7,15},{8,0},{9,1},... | collective-permute-start | bytes 884744 | tf_op jit(solution)/shard_map/ppermute | solution.py:657
  296.8 26.4 %collective-permute-start.17 = (bf16[2,96,768]{2,1,0:T(8,128)(2,1)S(1)}, bf16[2,96,768]{2,1,0:T(8,128)(2,1)S(1)}, u32[]{:S(2)}, u32[]{:S(2)}) collective-permute-start(bf16[2,96,768]{2,1,0:T(8,128)(2,1)S(1)} %get-tuple-element.158), channel_id=1, source_target_pairs={{0,8},{1,9},{2,10},{3,11},{4,12},{5,13},{6,14},{7,15},{8,0},{9,1},... | collective-permute-start | bytes 884744 | tf_op jit(solution)/shard_map/ppermute | solution.py:657
  307.5 17.5 %collective-permute-start.22 = (bf16[2,192,384]{2,1,0:T(8,128)(2,1)S(1)}, bf16[2,192,384]{2,1,0:T(8,128)(2,1)S(1)}, u32[]{:S(2)}, u32[]{:S(2)}) collective-permute-start(bf16[2,192,384]{2,1,0:T(8,128)(2,1)S(1)} %get-tuple-element.156), channel_id=1, source_target_pairs={{0,8},{1,9},{2,10},{3,11},{4,12},{5,13},{6,14},{7,15},{8,0},{9,1},... | collective-permute-start | bytes 884744 | tf_op jit(solution)/shard_map/ppermute | solution.py:657
  321.9 15.4 %copy-start.5 = (f32[96,576]{1,0:T(8,128)S(1)}, f32[96,576]{1,0:T(8,128)}, u32[]{:S(2)}) copy-start(f32[96,576]{1,0:T(8,128)} %param.26) | copy-start | bytes 663556
  321.9 15.4 %copy-start.12 = (f32[96,576]{1,0:T(8,128)S(1)}, f32[96,576]{1,0:T(8,128)}, u32[]{:S(2)}) copy-start(f32[96,576]{1,0:T(8,128)} %param.31) | copy-start | bytes 663556
  321.9 15.3 %collective-permute-start.13 = (bf16[96,768]{1,0:T(8,128)(2,1)S(1)}, bf16[96,768]{1,0:T(8,128)(2,1)S(1)}, u32[]{:S(2)}, u32[]{:S(2)}) collective-permute-start(bf16[96,768]{1,0:T(8,128)(2,1)S(1)} %fusion.29), channel_id=1, source_target_pairs={{0,16},{1,17},{2,18},{3,19},{4,20},{5,21},{6,22},{7,23},{8,24},{9,... | collective-permute-start | bytes 442376 | tf_op jit(solution)/shard_map/ppermute | solution.py:657
  323.2 17.9 %collective-permute-start.18 = (bf16[96,768]{1,0:T(8,128)(2,1)S(1)}, bf16[96,768]{1,0:T(8,128)(2,1)S(1)}, u32[]{:S(2)}, u32[]{:S(2)}) collective-permute-start(bf16[96,768]{1,0:T(8,128)(2,1)S(1)} %fusion.31), channel_id=1, source_target_pairs={{0,16},{1,17},{2,18},{3,19},{4,20},{5,21},{6,22},{7,23},{8,24},{9,... | collective-permute-start | bytes 442376 | tf_op jit(solution)/shard_map/ppermute | solution.py:657
  325.1 14.1 %copy-start.8 = (f32[96,192]{1,0:T(8,128)S(1)}, f32[96,192]{1,0:T(8,128)}, u32[]{:S(2)}) copy-start(f32[96,192]{1,0:T(8,128)} %param.27) | copy-start | bytes 221188
  325.1 14.1 %copy-start.16 = (f32[96,192]{1,0:T(8,128)S(1)}, f32[96,192]{1,0:T(8,128)}, u32[]{:S(2)}) copy-start(f32[96,192]{1,0:T(8,128)} %param.32) | copy-start | bytes 221188
  325.1 21.6 %collective-permute-start.23 = (bf16[192,384]{1,0:T(8,128)(2,1)S(1)}, bf16[192,384]{1,0:T(8,128)(2,1)S(1)}, u32[]{:S(2)}, u32[]{:S(2)}) collective-permute-start(bf16[192,384]{1,0:T(8,128)(2,1)S(1)} %fusion.33), channel_id=1, source_target_pairs={{0,16},{1,17},{2,18},{3,19},{4,20},{5,21},{6,22},{7,23},{8,24},{9,... | collective-permute-start | bytes 442376 | tf_op jit(solution)/shard_map/ppermute | solution.py:657
  339.2 19.4 %copy-start.6 = (f32[96,576]{1,0:T(8,128)}, f32[96,576]{1,0:T(8,128)S(1)}, u32[]{:S(2)}) copy-start(f32[96,576]{1,0:T(8,128)S(1)} %get-tuple-element.131) | copy-start | bytes 663556
  340.9 34.4 %copy-start.9 = (f32[96,192]{1,0:T(8,128)}, f32[96,192]{1,0:T(8,128)S(1)}, u32[]{:S(2)}) copy-start(f32[96,192]{1,0:T(8,128)S(1)} %get-tuple-element.134) | copy-start | bytes 221188
  341.0 5.7 %copy-start.2 = (f32[384,192]{0,1:T(8,128)S(1)}, f32[384,192]{0,1:T(8,128)}, u32[]{:S(2)}) copy-start(f32[384,192]{0,1:T(8,128)} %param.29) | copy-start | bytes 884740
  341.0 5.7 %copy-start.7 = (bf16[384,192]{0,1:T(8,128)(2,1)S(1)}, bf16[384,192]{0,1:T(8,128)(2,1)}, u32[]{:S(2)}) copy-start(bf16[384,192]{0,1:T(8,128)(2,1)} %copy.108) | copy-start | bytes 442372
  341.0 5.7 %copy-start.11 = (f32[384,192]{0,1:T(8,128)S(1)}, f32[384,192]{0,1:T(8,128)}, u32[]{:S(2)}) copy-start(f32[384,192]{0,1:T(8,128)} %param.34) | copy-start | bytes 884740
  341.0 14.2 %collective-permute-start.24 = (bf16[1,96,768]{2,1,0:T(8,128)(2,1)S(1)}, bf16[1,96,768]{2,1,0:T(8,128)(2,1)S(1)}, u32[]{:S(2)}, u32[]{:S(2)}) collective-permute-start(bf16[1,96,768]{2,1,0:T(8,128)(2,1)S(1)} %maximum_bitcast_fusion), channel_id=1, source_target_pairs={{0,16},{1,17},{2,18},{3,19},{4,20},{5,21},{6,22},{7,23},{8,24},{9,... | collective-permute-start | bytes 442376 | tf_op jit(solution)/shard_map/ppermute | solution.py:665
  343.1 15.4 %collective-permute-start.27 = (bf16[1,96,768]{2,1,0:T(8,128)(2,1)S(1)}, bf16[1,96,768]{2,1,0:T(8,128)(2,1)S(1)}, u32[]{:S(2)}, u32[]{:S(2)}) collective-permute-start(bf16[1,96,768]{2,1,0:T(8,128)(2,1)S(1)} %get-tuple-element.126), channel_id=1, source_target_pairs={{0,16},{1,17},{2,18},{3,19},{4,20},{5,21},{6,22},{7,23},{8,24},{9,... | collective-permute-start | bytes 442376 | tf_op jit(solution)/shard_map/ppermute | solution.py:665
  347.7 10.8 %copy-start.4 = (f32[384,192]{0,1:T(8,128)}, f32[384,192]{0,1:T(8,128)S(1)}, u32[]{:S(2)}) copy-start(f32[384,192]{0,1:T(8,128)S(1)} %get-tuple-element.125) | copy-start | bytes 884740
  348.5 20.5 %collective-permute-start.30 = (bf16[1,192,384]{2,1,0:T(8,128)(2,1)S(1)}, bf16[1,192,384]{2,1,0:T(8,128)(2,1)S(1)}, u32[]{:S(2)}, u32[]{:S(2)}) collective-permute-start(bf16[1,192,384]{2,1,0:T(8,128)(2,1)S(1)} %get-tuple-element.123), channel_id=1, source_target_pairs={{0,16},{1,17},{2,18},{3,19},{4,20},{5,21},{6,22},{7,23},{8,24},{9,... | collective-permute-start | bytes 442376 | tf_op jit(solution)/shard_map/ppermute | solution.py:665
  355.3 12.6 %collective-permute-start.25 = (bf16[2,96,768]{2,1,0:T(8,128)(2,1)S(1)}, bf16[2,96,768]{2,1,0:T(8,128)(2,1)S(1)}, u32[]{:S(2)}, u32[]{:S(2)}) collective-permute-start(bf16[2,96,768]{2,1,0:T(8,128)(2,1)S(1)} %pad_maximum_fusion.6), channel_id=1, source_target_pairs={{0,8},{1,9},{2,10},{3,11},{4,12},{5,13},{6,14},{7,15},{8,0},{9,1},... | collective-permute-start | bytes 884744 | tf_op jit(solution)/shard_map/ppermute | solution.py:665
  358.5 15.7 %collective-permute-start.28 = (bf16[2,96,768]{2,1,0:T(8,128)(2,1)S(1)}, bf16[2,96,768]{2,1,0:T(8,128)(2,1)S(1)}, u32[]{:S(2)}, u32[]{:S(2)}) collective-permute-start(bf16[2,96,768]{2,1,0:T(8,128)(2,1)S(1)} %pad_maximum_fusion.7), channel_id=1, source_target_pairs={{0,8},{1,9},{2,10},{3,11},{4,12},{5,13},{6,14},{7,15},{8,0},{9,1},... | collective-permute-start | bytes 884744 | tf_op jit(solution)/shard_map/ppermute | solution.py:665
  367.9 16.3 %collective-permute-start.26 = (bf16[4,96,768]{2,1,0:T(8,128)(2,1)S(1)}, bf16[4,96,768]{2,1,0:T(8,128)(2,1)S(1)}, u32[]{:S(2)}, u32[]{:S(2)}) collective-permute-start(bf16[4,96,768]{2,1,0:T(8,128)(2,1)S(1)} %pad_maximum_fusion.3), channel_id=1, source_target_pairs={{0,4},{1,5},{2,6},{3,7},{4,0},{5,1},{6,2},{7,3},{8,12},{9,13},{10,... | collective-permute-start | bytes 1769480 | tf_op jit(solution)/shard_map/ppermute | solution.py:665
  369.0 11.4 %collective-permute-start.31 = (bf16[2,192,384]{2,1,0:T(8,128)(2,1)S(1)}, bf16[2,192,384]{2,1,0:T(8,128)(2,1)S(1)}, u32[]{:S(2)}, u32[]{:S(2)}) collective-permute-start(bf16[2,192,384]{2,1,0:T(8,128)(2,1)S(1)} %pad_maximum_fusion.8), channel_id=1, source_target_pairs={{0,8},{1,9},{2,10},{3,11},{4,12},{5,13},{6,14},{7,15},{8,0},{9,1},... | collective-permute-start | bytes 884744 | tf_op jit(solution)/shard_map/ppermute | solution.py:665
  374.2 22.6 %collective-permute-start.29 = (bf16[4,96,768]{2,1,0:T(8,128)(2,1)S(1)}, bf16[4,96,768]{2,1,0:T(8,128)(2,1)S(1)}, u32[]{:S(2)}, u32[]{:S(2)}) collective-permute-start(bf16[4,96,768]{2,1,0:T(8,128)(2,1)S(1)} %pad_maximum_fusion.4), channel_id=1, source_target_pairs={{0,4},{1,5},{2,6},{3,7},{4,0},{5,1},{6,2},{7,3},{8,12},{9,13},{10,... | collective-permute-start | bytes 1769480 | tf_op jit(solution)/shard_map/ppermute | solution.py:665
  381.3 27.2 %collective-permute-start.32 = (bf16[4,192,384]{2,1,0:T(8,128)(2,1)}, bf16[4,192,384]{2,1,0:T(8,128)(2,1)}, u32[]{:S(2)}, u32[]{:S(2)}) collective-permute-start(bf16[4,192,384]{2,1,0:T(8,128)(2,1)} %pad_maximum_fusion.5), channel_id=1, source_target_pairs={{0,4},{1,5},{2,6},{3,7},{4,0},{5,1},{6,2},{7,3},{8,12},{9,13},{10,... | collective-permute-start | bytes 1769480 | tf_op jit(solution)/shard_map/ppermute | solution.py:665
  (12 other events, 30.7 us)
